TPU v7x, 128 devices: a whole 4x4x4 slice. The times are simulated.
128 devices in a mesh: batch: 2 (over x_hi), blk: 16 (over x_lo, z, core), ulysses: 4 (over y).
Axes of the slice: x: 4 (x_hi: 2, x_lo: 2; x = x_hi * 2 + x_lo), y: 4, z: 4, core: 2. Of those that a mesh axis runs over, the one named last changes fastest.
Arguments:
- tokens: bfloat16 [16384, 768], P(('batch', 'blk', 'ulysses')), may hold values from -6 to 6
- stretch_order: int32 [2, 32], P('batch'), may hold values from 0 to 31, each once within a row
- ln_gain: bfloat16 [1, 1536], P(None, ('batch', 'blk', 'ulysses')), may hold values from 0.5 to 1.5
- ln_bias: bfloat16 [1, 1536], P(None, ('batch', 'blk', 'ulysses')), may hold values from -3 to 3
- w_qkv: bfloat16 [1, 768, 2304], P(None, ('batch', 'blk', 'ulysses')), may hold values from -0.21875 to 0.21875
- qv_bias: bfloat16 [1, 1536], P(None, ('batch', 'blk', 'ulysses')), may hold values from -4 to 4
- w_out: bfloat16 [1, 768, 768], P(None, ('batch', 'blk', 'ulysses')), may hold values from -0.875 to 0.875
- out_bias: bfloat16 [1, 768], P(None, ('batch', 'blk', 'ulysses')), may hold values from -3 to 3
- w_up: bfloat16 [1, 768, 3072], P(None, ('batch', 'blk', 'ulysses')), may hold values from -0.21875 to 0.21875
- up_bias: bfloat16 [1, 3072], P(None, ('batch', 'blk', 'ulysses')), may hold values from -4 to 4
- w_down: bfloat16 [1, 3072, 768], P(None, ('batch', 'blk', 'ulysses')), may hold values from -0.21875 to 0.21875
- down_bias: bfloat16 [1, 768], P(None, ('batch', 'blk', 'ulysses')), may hold values from -3 to 3
- cotangent: float32 [16384, 768], P(('batch', 'blk', 'ulysses')), may hold values from -6 to 6
Outputs:
- result: float32 [16384, 768], P(('batch', 'blk', 'ulysses'))
- d_tokens: float32 [16384, 768], P(('batch', 'blk', 'ulysses'))
- g_ln_gain: float32 [1, 1536], P(None, ('batch', 'blk', 'ulysses'))
- g_ln_bias: float32 [1, 1536], P(None, ('batch', 'blk', 'ulysses'))
- g_w_qkv: float32 [1, 768, 2304], P(None, ('batch', 'blk', 'ulysses'))
- g_qv_bias: float32 [1, 1536], P(None, ('batch', 'blk', 'ulysses'))
- g_w_out: float32 [1, 768, 768], P(None, ('batch', 'blk', 'ulysses'))
- g_out_bias: float32 [1, 768], P(None, ('batch', 'blk', 'ulysses'))
- g_w_up: float32 [1, 768, 3072], P(None, ('batch', 'blk', 'ulysses'))
- g_up_bias: float32 [1, 3072], P(None, ('batch', 'blk', 'ulysses'))
- g_w_down: float32 [1, 3072, 768], P(None, ('batch', 'blk', 'ulysses'))
- g_down_bias: float32 [1, 768], P(None, ('batch', 'blk', 'ulysses'))
Inputs may be any that keep to these rules, and one draw needn't show every extreme that they name: Each row of stretch_order is a permutation of the 32 stretches of 256 positions; stored rows 2 j * 256 to 2 (j + 1) * 256 - 1 of a sequence hold the stretches named at entries 2 j and 2 j + 1, in that order.
All inputs are finite; a program needn't handle non-finite values.
Results may differ from a plain program's by a relative error of at most 0.038.
Values may be sent and summed in bfloat16 or wider, within the bound.
No kernel may reach another device: no remote copies, remote signals or barrier semaphores. Data moves between devices by JAX's collectives and lax.ppermute only.
A program may use at most 256 MiB of HBM per device.

v0:
```python
import functools
import math

import jax
import jax.numpy as jnp
from jax import lax
from jax.experimental import pallas as pl
from jax.experimental.pallas import tpu as pltpu
from jax.sharding import Mesh, PartitionSpec as P

HEADS = 12
HEAD_DIM = 64
NORM_EPS = 1e-05
FLOOR = -1e25
HIGHEST_ABOVE = 60.0
LANES = 256
EXTRA = 64
BELOW_FLOOR = -1e30
BLK = ("xlo", "z", "core")
CHIPS = ("batch", "xlo", "z")
WIDE = ("batch", "xlo", "z", "core")
ALL = ("batch", "xlo", "z", "core", "ulysses")
BF16 = jnp.bfloat16
F32 = jnp.float32
NT = (((1,), (1,)), ((), ()))
VMEM_LIMIT = 60 * 1024 * 1024


def mm(a, b):
    return jnp.dot(a, b, preferred_element_type=F32)


def mm_nt(a, b):
    return lax.dot_general(a, b, NT, preferred_element_type=F32)


def mm_tn(a, b):
    return lax.dot_general(a, b, (((0,), (0,)), ((), ())), preferred_element_type=F32)


def stretch(index, half):
    return pl.ds(pl.multiple_of(index * half, half), half)


def lanes_of(rows):
    return lax.broadcasted_iota(jnp.int32, (rows, LANES), 1)


def ones_after(k, first):
    return jnp.where(lanes_of(k.shape[0]) < first, k, jnp.ones_like(k))


def ones_before(v):
    return jnp.where(lanes_of(v.shape[0]) < EXTRA, jnp.ones_like(v), v)


def three(x):
    high = x.astype(BF16).astype(F32)
    mid = (x - high).astype(BF16).astype(F32)
    return high, mid, x - high - mid


def causal(half, heads, keys_first):
    rows = lax.broadcasted_iota(jnp.int32, (heads * half, half), 0) & (half - 1)
    cols = lax.broadcasted_iota(jnp.int32, (heads * half, half), 1)
    return rows <= cols if keys_first else cols <= rows


def merged_heads(stacked, half, heads, first):
    lane = lanes_of(half)
    out = stacked[:half]
    for h in range(1, heads):
        out = jnp.where(lane < first + h * HEAD_DIM, out, stacked[h * half : (h + 1) * half])
    return out


def in_groups(first, count, tiles):
    def eight(i, _):
        tiles([first + 8 * i + j for j in range(8)])
        return 0

    lax.fori_loop(0, count // 8, eight, 0)
    for size in (4, 2, 1):

        @pl.when((count & size) != 0)
        def _():
            begin = first + (count & ~(2 * size - 1))
            tiles([begin + j for j in range(size)])


def one_ahead(items, produce, consume):
    ready = produce(items[0])
    for n, item in enumerate(items):
        now = ready
        if n + 1 < len(items):
            ready = produce(items[n + 1])
        consume(item, now)


def attend_kernel(
    slots, own, q_heads, kv, ctx_low, ctx, lse, shift, total, q_ext, top, *, half, heads
):
    deep = heads * half
    lane = lanes_of(deep)

    def one_half(part, _):
        rank_own = own[part]
        mask = causal(half, heads, False)
        here = stretch(slots[rank_own], half)
        scores = jnp.where(mask, mm_nt(q_heads[part], kv[here, :LANES]), BELOW_FLOOR)
        first = jnp.max(scores, axis=1, keepdims=True).astype(BF16).astype(F32)
        shift[...] = first
        q_ext[...] = jnp.where(lane == heads * HEAD_DIM, -first, q_heads[part].astype(F32)).astype(
            BF16
        )
        top[...] = jnp.zeros_like(top)
        total[...] = mm(jnp.exp(scores - first).astype(BF16), ones_before(kv[here, 128:]))

        def tiles(ranks):
            at = [stretch(slots[r], half) for r in ranks]
            added = [total[...], top[...]]

            def produce(a):
                return mm_nt(q_ext[...], ones_after(kv[a, :LANES], heads * HEAD_DIM))

            def consume(a, above):
                added[1] = jnp.maximum(added[1], jnp.max(above.reshape(deep // 8, 8, half), axis=0))
                added[0] += mm(jnp.exp(above).astype(BF16), ones_before(kv[a, 128:]))

            one_ahead(at, produce, consume)
            total[...] = added[0]
            top[...] = added[1]

        in_groups(0, rank_own, tiles)

        @pl.when(jnp.logical_not(jnp.max(top[...]) < HIGHEST_ABOVE))
        def _():
            shift[...] = jnp.full_like(shift, FLOOR)
            total[...] = jnp.zeros_like(total)

            def again(rank, _):
                a = stretch(slots[rank], half)
                allowed = jnp.logical_or(mask, rank < rank_own)
                scores = jnp.where(allowed, mm_nt(q_heads[part], kv[a, :LANES]), BELOW_FLOOR)
                new = jnp.maximum(shift[...], jnp.max(scores, axis=1, keepdims=True))
                total[...] = total[...] * jnp.exp(shift[...] - new) + mm(
                    jnp.exp(scores - new).astype(BF16), ones_before(kv[a, 128:])
                )
                shift[...] = new
                return 0

            lax.fori_loop(0, rank_own + 1, again, 0)

        row_sum = total[:, :1]
        lse[part] = shift[...] + jnp.log(row_sum)
        done = merged_heads(total[...] / row_sum, half, heads, EXTRA)
        rows = stretch(part, half)
        ctx[rows, :] = done
        ctx_low[:, rows] = done.T[EXTRA:, :].astype(BF16)
        return 0

    lax.fori_loop(0, 2, one_half, 0)


def query_grad_kernel(slots, own, q_ext, d_ext, kv, d_query, total, *, half, heads):
    def one_half(part, _):
        rank_own = own[part]
        total[...] = jnp.zeros_like(total)

        def tiles(ranks, mask=None):
            at = [stretch(slots[r], half) for r in ranks]
            added = [total[...]]

            def produce(a):
                return (
                    mm_nt(q_ext[part], ones_after(kv[a, :LANES], heads * HEAD_DIM)),
                    mm_nt(d_ext[part], ones_before(kv[a, 128:])),
                )

            def consume(a, ready):
                probs = jnp.exp(ready[0])
                if mask is not None:
                    probs = jnp.where(mask, probs, 0.0)
                added[0] += mm((probs * ready[1]).astype(BF16), kv[a, :LANES])

            one_ahead(at, produce, consume)
            total[...] = added[0]

        in_groups(0, rank_own, tiles)
        tiles([rank_own], causal(half, heads, False))
        done = merged_heads(total[...], half, heads, 0)
        d_query[stretch(part, half), :] = (done * (1.0 / math.sqrt(HEAD_DIM))).astype(BF16)
        return 0

    lax.fori_loop(0, 2, one_half, 0)


def key_grad_kernel(
    slots, own, k_heads, v_heads, q_all, p_all, d_key, d_value, k_sum, v_sum, *, half, heads
):
    count = slots.shape[0]
    lane = lanes_of(half)

    def one_half(part, _):
        rank_own = own[part]
        k_sum[...] = jnp.zeros_like(k_sum)
        v_sum[...] = jnp.zeros_like(v_sum)

        def tiles(ranks, mask=None):
            at = [stretch(slots[r], half) for r in ranks]
            added = [k_sum[...], v_sum[...]]

            def produce(a):
                return (
                    mm_nt(k_heads[part], jnp.where(lane < EXTRA, p_all[a, :], q_all[a, :])),
                    mm_nt(v_heads[part], p_all[a, :]),
                )

            def consume(a, ready):
                probs = jnp.exp(ready[0])
                if mask is not None:
                    probs = jnp.where(mask, probs, 0.0)
                added[1] += mm(probs.astype(BF16), p_all[a, :])
                added[0] += mm((probs * ready[1]).astype(BF16), q_all[a, :])

            one_ahead(at, produce, consume)
            k_sum[...], v_sum[...] = added

        tiles([rank_own], causal(half, heads, True))
        in_groups(rank_own + 1, count - 1 - rank_own, tiles)
        rows = stretch(part, half)
        d_key[rows, :] = merged_heads(k_sum[...], half, heads, EXTRA).astype(BF16)
        d_value[rows, :] = merged_heads(v_sum[...], half, heads, EXTRA)[:, EXTRA:].astype(BF16)
        return 0

    lax.fori_loop(0, 2, one_half, 0)


def prepare_kernel(dc, w_out, ctx, lse, q_heads, packed, q_ext, d_ext, *, half, heads):
    lane = lanes_of(half)
    d_ctx = mm_nt(dc[...], w_out[...]).astype(BF16)
    for part in range(2):
        rows = slice(part * half, (part + 1) * half)
        grads = d_ctx[rows, :]
        terms = grads.astype(F32) * ctx[rows, :]
        extra = grads.astype(F32)
        for h in range(heads):
            deep = slice(h * half, (h + 1) * half)
            first = EXTRA + h * HEAD_DIM
            here = jnp.logical_and(lane >= first, lane < first + HEAD_DIM)
            delta = jnp.sum(jnp.where(here, terms, 0.0), axis=1, keepdims=True)
            minus_lse = three(-lse[part, deep, :])
            minus_delta = three(-delta)
            q_new = q_heads[part, deep, :].astype(F32)
            d_new = jnp.where(here, grads.astype(F32), 0.0)
            for i in range(3):
                q_new = jnp.where(lane == heads * HEAD_DIM + i, minus_lse[i], q_new)
                d_new = jnp.where(lane == i, minus_delta[i], d_new)
                extra = jnp.where(lane == 3 * h + i, minus_lse[i], extra)
                extra = jnp.where(lane == 3 * (heads + h) + i, minus_delta[i], extra)
            q_ext[part, deep, :] = q_new.astype(BF16)
            d_ext[part, deep, :] = d_new.astype(BF16)
        packed[rows, :] = extra.astype(BF16)


def project_kernel(me, x, weights, h1, n1, kv, q, vec, bias, *, wide, ways, pair, part):
    count = ways * pair
    each = weights.shape[0] // wide
    for w in range(wide):
        block = weights[w * each : w * each + 8, 512:].astype(F32)
        vec[:, w * count : (w + 1) * count] = block[:, 64 : 64 + count]
    width = x.shape[1]
    bias[...] = jnp.zeros_like(bias)
    for u in range(ways):

        @pl.when(me[0] == u)
        def _():
            bias[0:1, :part] = vec[2:3, u * part : (u + 1) * part]
            bias[0:1, 2 * part : 3 * part] = vec[2:3, width + u * part : width + (u + 1) * part]

    normed, _ = normalized(x[...].astype(F32))
    n1[...] = normed
    h1_low = (normed * vec[0:1, :width] + vec[1:2, :width]).astype(BF16)
    h1[...] = h1_low
    proj = (mm(h1_low, weights[...]) + bias[0:1, :]).astype(BF16)
    q[...] = proj[:, :part] * jnp.asarray(1.0 / math.sqrt(HEAD_DIM), BF16)
    kv[...] = proj[:, part : 3 * part]


def project(me, both, weights, part, wide, ways, pair):
    rows = both.shape[0]
    width = both.shape[1] // 2
    outs = [
        ((rows, width), BF16),
        ((rows, width), F32),
        ((rows, 2 * part), BF16),
        ((rows, part), BF16),
        ((8, wide * ways * pair), F32),
    ]
    return pl.pallas_call(
        functools.partial(project_kernel, wide=wide, ways=ways, pair=pair, part=part),
        out_shape=tuple(jax.ShapeDtypeStruct(s, t) for s, t in outs),
        grid_spec=pltpu.PrefetchScalarGridSpec(
            num_scalar_prefetch=1,
            grid=(1,),
            in_specs=[pl.BlockSpec((rows, width), lambda i, *_: (0, 0)), whole(weights.shape)],
            out_specs=[whole(s) for s, _ in outs],
            scratch_shapes=[pltpu.VMEM((8, weights.shape[1]), F32)],
        ),
        compiler_params=params(),
        cost_estimate=pl.CostEstimate(
            flops=2 * rows * weights.size, bytes_accessed=8 * rows * width, transcendentals=rows
        ),
        name="project",
    )(me, both, weights)


def finish_kernel(
    core, me, d_query, d_key, d_value, h1, n1, weights, small, terms, kept, sent, d_proj, g, rows_of
):
    chips, deep, _ = kept.shape
    lane = lax.broadcasted_iota(jnp.int32, (d_query.shape[0], 128), 1)
    part = d_value.shape[1]
    d_proj[:, :128] = d_query[:, :128]
    d_proj[:, 128:256] = jnp.where(lane < EXTRA, d_query[:, 128:], d_key[:, :128])
    d_proj[:, 256:384] = d_key[:, 128:]
    d_proj[:, 512:] = jnp.zeros_like(d_proj[:, 512:])
    d_proj[:, 384 : 384 + part] = d_value[...]
    dh1 = mm_nt(d_proj[...], weights[...])
    terms[...] = dh1.astype(BF16)
    g[...] = mm_tn(h1[...], d_proj[...])
    gain_row = jnp.sum(dh1 * n1[...], axis=0, keepdims=True)
    shift_row = jnp.sum(dh1, axis=0, keepdims=True)
    sums = jnp.sum(d_proj[...].astype(F32), axis=0, keepdims=True)
    rows_of[...] = small[...]
    count = 2 * chips
    each = h1.shape[1] // count
    wide = 2 * each
    for w in range(count // 2):
        rows_of[w, 0:1, :wide] = gain_row[:, w * wide : (w + 1) * wide]
        rows_of[w, 1:2, :wide] = shift_row[:, w * wide : (w + 1) * wide]
    many = part // wide
    for i in range(many):
        at = many * me[0] + i
        rows_of[at, 2:3, :wide] = sums[:, i * wide : (i + 1) * wide]
        rows_of[count // 2 + at, 2:3, :wide] = sums[:, 384 + i * wide : 384 + (i + 1) * wide]

    def put(target, which):
        target[:, each:, 128:] = jnp.zeros((chips, deep - each, target.shape[2] - 128), target.dtype)
        for c in range(chips):
            w = 2 * c + which
            target[c, :each, :] = g[w * each : (w + 1) * each, :].astype(target.dtype)
            target[c, each:, :128] = rows_of[w].astype(target.dtype)

    for which in range(2):

        @pl.when(core[0] == which)
        def _():
            put(kept, which)
            put(sent, 1 - which)


def finish(core, me, d_query, d_key, d_value, h1, n1, weights, small):
    rows, width = h1.shape
    count = small.shape[0]
    shape = (count // 2, width // count + 8, weights.shape[1])
    return call(
        finish_kernel, "finish", (core, me), (d_query, d_key, d_value, h1, n1, weights, small),
        [((rows, width), BF16), (shape, F32), (shape, BF16)],
        [((rows, weights.shape[1]), BF16), ((width, weights.shape[1]), F32), (small.shape, F32)],
        pl.CostEstimate(flops=4 * weights.size * rows, bytes_accessed=6 * weights.size, transcendentals=0),
    )


def whole(shape):
    return pl.BlockSpec(shape, lambda i, *_: (0,) * len(shape))


def params():
    return pltpu.CompilerParams(
        dimension_semantics=("arbitrary",), vmem_limit_bytes=VMEM_LIMIT
    )


def cost(rows, keys, heads, products):
    area = rows * keys * heads
    return pl.CostEstimate(
        flops=2 * area * 256 * products, bytes_accessed=keys * 768, transcendentals=area
    )


def call(kernel, name, scalars, arrays, outs, scratch, estimate, **static):
    return pl.pallas_call(
        functools.partial(kernel, **static),
        out_shape=tuple(jax.ShapeDtypeStruct(s, t) for s, t in outs),
        grid_spec=pltpu.PrefetchScalarGridSpec(
            num_scalar_prefetch=len(scalars),
            grid=(1,),
            in_specs=[whole(a.shape) for a in arrays],
            out_specs=[whole(s) for s, _ in outs],
            scratch_shapes=[pltpu.VMEM(s, t) for s, t in scratch],
        ),
        compiler_params=params(),
        cost_estimate=estimate,
        name=name,
    )(*scalars, *arrays)


def attend(slots, own, q_heads, kv, heads):
    _, deep, _ = q_heads.shape
    half = deep // heads
    width = heads * HEAD_DIM
    return call(
        attend_kernel, "attend", (slots, own), (q_heads, kv),
        [((width, 2 * half), BF16), ((2 * half, LANES), F32), ((2, deep, 1), F32)],
        [((deep, 1), F32), ((deep, LANES), F32), ((deep, LANES), BF16), ((8, half), F32)],
        cost(2 * half, kv.shape[0], heads, 2), half=half, heads=heads,
    )


def prepare(dc, w_out, ctx, lse, q_heads, heads):
    _, deep, _ = q_heads.shape
    half = deep // heads
    return call(
        prepare_kernel, "prepare", (), (dc, w_out, ctx, lse, q_heads),
        [((2 * half, LANES), BF16), (q_heads.shape, BF16), (q_heads.shape, BF16)], [],
        pl.CostEstimate(flops=2 * dc.size * LANES, bytes_accessed=4 * q_heads.size, transcendentals=0),
        half=half, heads=heads,
    )


def query_grad(slots, own, q_ext, d_ext, kv, heads):
    _, deep, _ = q_ext.shape
    half = deep // heads
    return call(
        query_grad_kernel, "query_grad", (slots, own), (q_ext, d_ext, kv),
        [((2 * half, LANES), BF16)], [((deep, LANES), F32)],
        cost(2 * half, kv.shape[0], heads, 3), half=half, heads=heads,
    )[0]


def key_grad(slots, own, k_heads, v_heads, q_all, p_all, heads):
    _, deep, _ = k_heads.shape
    half = deep // heads
    return call(
        key_grad_kernel, "key_grad", (slots, own), (k_heads, v_heads, q_all, p_all),
        [((2 * half, LANES), BF16), ((2 * half, heads * HEAD_DIM), BF16)], [((deep, LANES), F32)] * 2,
        cost(2 * half, q_all.shape[0], heads, 4), half=half, heads=heads,
    )


def feed_forward_kernel(
    me, x, ctx, df, vectors, w_up, w_out, w_down, x2_own, h2, act, du, dh2, down
):
    total = x[...].astype(F32) + vectors[2:3, :] + mm_tn(ctx[...], w_out[...])

    @pl.when(pl.program_id(0) == me[0])
    def _():
        x2_own[...] = total

    normed, _ = normalized(total)
    h2_low = (normed * vectors[0:1, :] + vectors[1:2, :]).astype(BF16)
    h2[...] = h2_low
    up = mm(h2_low, w_up[...]) + vectors[3:4, :]
    bend = math.sqrt(2.0 / math.pi)
    square = up * up
    turn = jnp.tanh(bend * (up + 0.044715 * square * up))
    half = 0.5 * (1.0 + turn)
    act_low = (up * half).astype(BF16)
    act[...] = act_low
    down[...] = mm(act_low, w_down[...]).astype(BF16)
    slope = half + 0.5 * up * (1.0 - turn * turn) * (bend * (1.0 + 3 * 0.044715 * square))
    du_low = (slope * mm_nt(df[...], w_down[...])).astype(BF16)
    du[...] = du_low
    dh2[...] = mm_nt(du_low, w_up[...]).astype(BF16)


def feed_forward(me, both, ctx, vectors, weights, ways):
    rows = both.shape[0]
    width = both.shape[1] // 2
    step = rows // ways

    def along(c):
        return pl.BlockSpec((step, width), lambda i, *_: (i, c))

    def third(c):
        return pl.BlockSpec((weights.shape[0], width), lambda i, *_: (0, c))

    flat = jax.ShapeDtypeStruct((rows, width), BF16)
    return pl.pallas_call(
        feed_forward_kernel,
        out_shape=(jax.ShapeDtypeStruct((step, width), F32), flat, flat, flat, flat, flat),
        grid_spec=pltpu.PrefetchScalarGridSpec(
            num_scalar_prefetch=1,
            grid=(ways,),
            in_specs=[
                along(0),
                pl.BlockSpec((width, step), lambda i, *_: (0, i)),
                along(1),
                whole(vectors.shape),
                third(0),
                third(1),
                third(2),
            ],
            out_specs=[whole((step, width))] + [along(0)] * 5,
        ),
        compiler_params=params(),
        cost_estimate=pl.CostEstimate(
            flops=10 * rows * width * width, bytes_accessed=6 * width * width, transcendentals=rows * width
        ),
        name="feed_forward",
    )(me, both, ctx, both, vectors, weights, weights, weights)


def weight_grads_kernel(core, h2, du, act, df, ctx, dc, kept, sent, g_up, g_down, g_out):
    chips, rows, width = kept.shape
    each = h2.shape[1] // (2 * chips)
    few = ctx.shape[0] // (2 * chips)
    chunk = h2.shape[1] // 2
    for i in range(2):
        cols = slice(i * chunk, (i + 1) * chunk)
        g_up[cols, :] = mm_tn(h2[:, cols], du[...])
        g_down[cols, :] = mm_tn(act[:, cols], df[...])
    g_out[...] = mm(ctx[...], dc[...])

    def put(target, which):
        kind = target.dtype
        target[:, 2 * each :, :] = jnp.zeros((chips, rows - 2 * each, width), kind)
        for c in range(chips):
            w = 2 * c + which
            target[c, :each, :] = g_up[w * each : (w + 1) * each, :].astype(kind)
            target[c, each : 2 * each, :] = g_down[w * each : (w + 1) * each, :].astype(kind)
            target[c, 2 * each : 2 * each + few, :] = g_out[w * few : (w + 1) * few, :].astype(kind)

    for which in range(2):

        @pl.when(core[0] == which)
        def _():
            put(kept, which)
            put(sent, 1 - which)


def weight_grads(core, h2, du, act, both, ctx, dc, owners):
    count, width = du.shape
    units = h2.shape[1]
    shape = (owners // 2, 2 * units // owners + 8, width)
    return pl.pallas_call(
        weight_grads_kernel,
        out_shape=(jax.ShapeDtypeStruct(shape, F32), jax.ShapeDtypeStruct(shape, BF16)),
        grid_spec=pltpu.PrefetchScalarGridSpec(
            num_scalar_prefetch=1,
            grid=(1,),
            in_specs=[
                whole(h2.shape),
                whole(du.shape),
                whole(act.shape),
                pl.BlockSpec((count, width), lambda i, *_: (0, 1)),
                whole(ctx.shape),
                whole(dc.shape),
            ],
            out_specs=[whole(shape)] * 2,
            scratch_shapes=[
                pltpu.VMEM((units, width), F32),
                pltpu.VMEM((units, width), F32),
                pltpu.VMEM((ctx.shape[0], width), F32),
            ],
        ),
        compiler_params=params(),
        cost_estimate=pl.CostEstimate(
            flops=4 * h2.size * width, bytes_accessed=6 * units * width, transcendentals=0
        ),
        name="weight_grads",
    )(core, h2, du, act, both, ctx, dc)


def normalized(values):
    mean = jnp.mean(values, axis=-1, keepdims=True)
    centered = values - mean
    spread = jnp.mean(centered * centered, axis=-1, keepdims=True)
    scale = lax.rsqrt(spread + NORM_EPS)
    return centered * scale, scale


def norm_back(grad, gain, normed, scale):
    e = grad * gain
    mean_e = jnp.mean(e, axis=-1, keepdims=True)
    mean_en = jnp.mean(e * normed, axis=-1, keepdims=True)
    return scale * (e - mean_e - normed * mean_en)


def gelu_tanh(values):
    return jax.nn.gelu(values, approximate=True)


def head_lanes(x, heads, first, ones_at=None):
    rows, width = x.shape
    wide = jnp.pad(x, ((0, 0), (first, LANES - width - first))).reshape(2, 1, rows // 2, LANES)
    lane = lax.broadcasted_iota(jnp.int32, (1, heads, 1, LANES), 3)
    head = lax.broadcasted_iota(jnp.int32, (1, heads, 1, LANES), 1)
    start = first + head * HEAD_DIM
    here = jnp.logical_and(lane >= start, lane < start + HEAD_DIM)
    out = jnp.where(here, wide, jnp.zeros((), x.dtype))
    if ones_at is not None:
        at = ones_at + 3 * head
        out = jnp.where(jnp.logical_and(lane >= at, lane < at + 3), jnp.ones((), x.dtype), out)
    return out.reshape(2, heads * rows // 2, LANES)


def to_all(x, axis="ulysses"):
    ways = lax.axis_size(axis)
    sent = jnp.broadcast_to(x[None], (ways,) + x.shape)
    return lax.all_to_all(sent, axis, split_axis=0, concat_axis=0, tiled=True)


def summed_at_owner(x, axis="ulysses"):
    ways = lax.axis_size(axis)
    sent = x.astype(BF16).reshape(ways, -1, x.shape[1])
    got = lax.all_to_all(sent, axis, split_axis=0, concat_axis=0, tiled=True)
    return jnp.sum(got.astype(F32), axis=0)


def other_core(x):
    return lax.ppermute(x, "core", [(0, 1), (1, 0)])


def reduced(x, axis):
    ways = lax.axis_size(axis)
    me = lax.axis_index(axis)

    def rows_of(k):
        return lax.dynamic_index_in_dim(x, lax.rem(me + k, ways), axis=0, keepdims=False)

    got = [
        lax.ppermute(rows_of(k).astype(BF16), axis, [(i, (i + k) % ways) for i in range(ways)])
        for k in range(1, ways)
    ]
    total = rows_of(0).astype(F32)
    for g in got:
        total += g.astype(F32)
    return total


def on_device(
    tokens,
    stretch_order,
    ln_gain,
    ln_bias,
    w_qkv,
    qv_bias,
    w_out,
    out_bias,
    w_up,
    up_bias,
    w_down,
    down_bias,
    cotangent,
):
    own_rows, width = tokens.shape
    ways = lax.axis_size("ulysses")
    wide = lax.axis_size(WIDE)
    me = lax.axis_index("ulysses")
    rows = own_rows * ways
    heads = HEADS // ways
    part = width // ways
    held = w_qkv.shape[1]
    ff_held = w_down.shape[1]
    ff_part = ff_held * wide
    pair = 2 * held

    order = stretch_order[0]
    own = lax.dynamic_slice(order, (2 * lax.axis_index(BLK),), (2,))
    count = order.shape[0]
    index = jnp.arange(count, dtype=jnp.int32)
    slots = jnp.sum(jnp.where(order[None, :] == index[:, None], index[None, :], 0), axis=1)

    small = jnp.concatenate(
        [
            ln_gain,
            ln_bias,
            qv_bias,
            jnp.concatenate([out_bias, down_bias], axis=1),
            up_bias.reshape(2, pair),
        ],
        axis=0,
    )
    qkv_slices = w_qkv[0].reshape(held, 3, ways, part).transpose(2, 0, 1, 3).reshape(ways, held, 3 * part)
    up_slices = w_up[0].reshape(held, wide, ways, ff_held).transpose(2, 0, 1, 3).reshape(ways, held, ff_part)
    first = jnp.concatenate(
        [
            qkv_slices,
            jnp.broadcast_to(small[None], (ways,) + small.shape),
            jnp.zeros((ways, held, width - 3 * part - pair), BF16),
        ],
        axis=2,
    )
    blank = jnp.zeros((ways, 8 - held, width), BF16)
    wide_out = jnp.broadcast_to(w_out[0][None], (ways, held, width))
    sent = jnp.concatenate([first, blank, up_slices, blank, wide_out, blank], axis=1)
    sent, tokens_late, cotangent_late = lax.optimization_barrier((sent, tokens, cotangent))
    got = lax.all_to_all(sent, "ulysses", split_axis=0, concat_axis=0, tiled=True)
    df_own = cotangent_late.astype(BF16)
    both = lax.all_gather(
        jnp.concatenate([tokens_late, df_own], axis=1), "ulysses", axis=0, tiled=True
    )
    matrix = got[:, :held, : 3 * part].reshape(ways * held, 3 * part)
    vector = got[:, :held, 3 * part : 3 * part + pair].transpose(1, 0, 2).reshape(held, ways * pair)
    vector = jnp.pad(vector, ((0, (ways - 1) * held), (0, 64 - ways * pair)))
    piece = jnp.concatenate([matrix, vector], axis=1)
    filled = lax.all_gather(piece, WIDE, axis=0, tiled=True)
    ffn = jnp.concatenate(
        [
            got[:, 8 : 8 + held].reshape(ways * held, width),
            got[:, 16 : 16 + held].reshape(ways * held, width),
            w_down[0],
        ],
        axis=1,
    )
    h1, n1, kv, q_scaled, vec = project(me[None], both, filled, part, wide, ways, pair)
    gains, shifts = vec[0], vec[1]
    halves = vec[3].reshape(wide * ways, 2, held)
    out_bias_all = halves[:, 0].reshape(-1)
    down_bias_all = halves[:, 1].reshape(-1)
    up_bias_u = lax.dynamic_index_in_dim(
        vec[4:6].reshape(2, wide, ways, pair), me, axis=2, keepdims=False
    )
    up_bias_u = up_bias_u.transpose(1, 0, 2).reshape(-1)
    kv_all = lax.all_gather(kv, BLK, axis=0, tiled=True)
    q_heads = head_lanes(q_scaled, heads, 0)
    k_heads = head_lanes(kv[:, :part], heads, EXTRA, 0)
    v_heads = head_lanes(kv[:, part:], heads, EXTRA, 3 * heads)
    q_wide = jnp.pad(q_scaled, ((0, 0), (EXTRA, 0)))
    gain_two = gains[width:]
    vectors = jnp.stack(
        [gain_two, shifts[width:], out_bias_all, up_bias_u] + [jnp.zeros((width,), F32)] * 4
    )
    (ffn, kv_all, slots, own, q_heads, k_heads, v_heads, q_wide, vectors, n1) = (
        lax.optimization_barrier(
            (ffn, kv_all, slots, own, q_heads, k_heads, v_heads, q_wide, vectors, n1)
        )
    )
    ffn_all = lax.all_gather(ffn, WIDE, axis=0, tiled=True)

    ctx_low, ctx, lse = attend(slots, own, q_heads, kv_all, heads)
    ctx_all = to_all(ctx_low).reshape(width, rows)
    q_wide, ctx_all = lax.optimization_barrier((q_wide, ctx_all))
    q_all = lax.all_gather(q_wide, BLK, axis=0, tiled=True)
    x2_own, h2, act, du, dh2, down = feed_forward(
        me[None], both, ctx_all, vectors, ffn_all, ways
    )
    dh2 = summed_at_owner(dh2)
    ctx_rows = lax.dynamic_index_in_dim(
        ctx_all.reshape(wide, ways, held, rows), me, axis=1, keepdims=False
    ).reshape(part, rows)
    w_out_u = lax.dynamic_slice(ffn_all, (me * part, width), (part, width))
    g_up_bias = jnp.sum(du.astype(F32), axis=0)
    g_down_bias = jnp.sum(df_own.astype(F32), axis=0)

    n2_own, r2_own = normalized(x2_own)
    dx2 = cotangent + norm_back(dh2, gain_two, n2_own, r2_own)
    g_gain_two = jnp.sum(dh2 * n2_own, axis=0)
    g_shift_two = jnp.sum(dh2, axis=0)
    dc_own = dx2.astype(BF16)
    g_out_bias = jnp.sum(dc_own.astype(F32), axis=0)
    owners = wide * ways
    blank = jnp.zeros((width,), F32)
    small_grads = jnp.stack(
        [
            jnp.concatenate([blank, g_gain_two]).reshape(wide, -1),
            jnp.concatenate([blank, g_shift_two]).reshape(wide, -1),
            jnp.zeros((wide, ways * pair), F32),
            jnp.concatenate(
                [g_out_bias.reshape(owners, held), g_down_bias.reshape(owners, held)], axis=1
            ).reshape(wide, -1),
        ],
        axis=1,
    )
    g_up_full = jnp.zeros((wide, 2, ways, pair), F32)
    g_up_full = lax.dynamic_update_slice(
        g_up_full, g_up_bias.reshape(wide, 2, 1, pair), (0, 0, me, 0)
    )
    small_grads = jnp.concatenate([small_grads, g_up_full.reshape(wide, 2, ways * pair)], axis=1)
    small_grads = jnp.pad(small_grads, ((0, 0), (0, 2), (0, 128 - ways * pair)))
    dc = to_all(dc_own).reshape(rows, width)
    dc, q_all, small_grads, ctx_rows = lax.optimization_barrier((dc, q_all, small_grads, ctx_rows))
    w_out_u = lax.dynamic_slice(ffn_all, (me * part, width), (part, width))

    w_out_wide = jnp.pad(w_out_u, ((EXTRA, 0), (0, 0)))
    packed, q_ext, d_ext = prepare(dc, w_out_wide, ctx, lse, q_heads, heads)
    packed_all = lax.all_gather(packed, BLK, axis=0, tiled=True)
    core = lax.axis_index("core")
    early, early_sent = weight_grads(core[None], h2, du, act, both, ctx_rows, dc, wide)
    early = (early + other_core(early_sent).astype(F32)).astype(BF16)
    early, q_ext = lax.optimization_barrier((early, q_ext))
    d_query = query_grad(slots, own, q_ext, d_ext, kv_all, heads)
    early, packed_all, d_query = lax.optimization_barrier((early, packed_all, d_query))
    early = lax.all_to_all(early, CHIPS, split_axis=0, concat_axis=0, tiled=True)
    d_key, d_value = key_grad(slots, own, k_heads, v_heads, q_all, packed_all, heads)
    early, d_value = lax.optimization_barrier((early, d_value))
    early = jnp.sum(early.astype(F32), axis=0)
    terms, late, late_sent = finish(
        core[None], me[None], d_query, d_key, d_value, h1, n1, filled, small_grads
    )
    terms, late_got = lax.optimization_barrier((terms, other_core(late_sent)))
    pair_sums = reduced(
        jnp.concatenate([terms, down], axis=1).reshape(ways, own_rows, 2 * width), "ulysses"
    )
    dh1 = pair_sums[:, :width]
    result = pair_sums[:, width:] + x2_own + down_bias_all
    late = (late + late_got.astype(F32)).astype(BF16)
    late = lax.all_to_all(late, CHIPS, split_axis=0, concat_axis=0, tiled=True)
    late = jnp.sum(late.astype(F32), axis=0)
    n1_own, r1_own = normalized(tokens.astype(F32))
    d_tokens = dx2 + norm_back(dh1, gains[:width], n1_own, r1_own)

    small_rows = late[ways * held : ways * held + 6, : ways * pair].reshape(6, ways, pair)
    last = jnp.concatenate(
        [
            late[: ways * held, : 3 * part].reshape(ways, held, 3 * part),
            jnp.pad(small_rows.transpose(1, 0, 2), ((0, 0), (0, 0), (0, 64 - pair))),
            early[:ff_held].reshape(ways, held, -1),
        ],
        axis=2,
    )
    last = lax.all_to_all(last, "ulysses", split_axis=0, concat_axis=0, tiled=True)
    o_w_qkv = last[:, :, : 3 * part].reshape(ways, held, 3, part).transpose(1, 2, 0, 3)
    o_small = jnp.sum(last[:, :, 3 * part : 3 * part + pair], axis=0)
    o_w_up = last[:, :, 3 * part + 64 :].reshape(ways, held, wide, ff_held).transpose(1, 2, 0, 3)
    return (
        result,
        d_tokens,
        o_small[0:1],
        o_small[1:2],
        o_w_qkv.reshape(1, held, 3 * width),
        o_small[2:3],
        early[None, 2 * ff_held : 2 * ff_held + held],
        o_small[3:4, :held],
        o_w_up.reshape(1, held, -1),
        o_small[4:6].reshape(1, ff_held),
        early[None, ff_held : 2 * ff_held],
        o_small[3:4, held:],
    )


def solution(mesh):
    chips_z = mesh.shape["blk"] // 4
    parts = Mesh(
        mesh.devices.reshape(mesh.shape["batch"], 2, chips_z, 2, mesh.shape["ulysses"]), ALL
    )
    rows = P(ALL, None)
    flat = P(None, ALL)
    deep = P(None, ALL, None)
    return jax.shard_map(
        on_device,
        mesh=parts,
        in_specs=(
            rows, P("batch", None), flat, flat, deep, flat, deep, flat, deep, flat, deep, flat, rows,
        ),
        out_specs=(rows, rows, flat, flat, deep, flat, deep, flat, deep, flat, deep, flat),
        check_vma=False,
    )
```

profile of v0, /device:TPU:0, one launch (start us, length us, event | category | flops | bytes accessed | tf_op | source)
XLA Modules:
  0.0 332.9 jit_solution(3849484123596967748)
XLA Ops:
  7.2 1.2 reshape_squeeze.10
  8.7 0.9 reshape_squeeze.9
  10.2 1.3 reduce.18
  15.6 4.5 %all-to-all-start = ((bf16[4,24,768]{2,1,0:T(8,128)(2,1)}), bf16[4,24,768]{2,1,0:T(8,128)(2,1)S(1)}, u32[]{:S(2)}, u32[]{:S(2)}) async-start(bf16[4,24,768]{2,1,0:T(8,128)(2,1)} %copy.86), calls=%async_computation | async-start | bytes 294912 | tf_op jit(solution)/shard_map/all_to_all | solution.py:700
  20.1 6.1 %all-to-all-done = bf16[4,24,768]{2,1,0:T(8,128)(2,1)S(1)} async-done(((bf16[4,24,768]{2,1,0:T(8,128)(2,1)}), bf16[4,24,768]{2,1,0:T(8,128)(2,1)S(1)}, u32[]{:S(2)}, u32[]{:S(2)}) %all-to-all-start) | async-done | bytes 147488 | tf_op jit(solution)/shard_map/all_to_all | solution.py:700
  26.5 28.5 %all_gather.19.weights = bf16[768,640]{1,0:T(8,128)(2,1)} all-gather(bf16[24,640]{1,0:T(8,128)(2,1)S(1)} %fusion.16), channel_id=1, replica_groups=mesh['batch'=2,'xlo'=2,'z'=4,'core'=2,'ulysses'=4] {'batch','xlo','z','c..., dimensions={0}, use_global_device_ids=true | all-gather | bytes 1013760 | tf_op jit(solution)/shard_map/all_gather | solution.py:709
  55.0 3.8 %project.1 = (bf16[512,768]{1,0:T(8,128)(2,1)}, f32[512,768]{1,0:T(8,128)}, bf16[512,384]{1,0:T(8,128)(2,1)}, bf16[512,192]{1,0:T(8,128)(2,1)}, f32[8,1536]{1,0:T(8,128)}) custom-call(s32[1]{0:T(128)} %bitcast.1.me, bf16[512,1536]{1,0:T(8,128)(2,1)} %all-gather.6.cloned.1.call-done.x.df, bf16[768,640]{1,0:T(8,128)(2,1)} %all_gather.19.weights), custom_call_target="tpu_custom_call" | custom-call | flops 503316480 | bytes 3145728 | tf_op jit(solution)/shard_map/project/pallas_call | solution.py:300
  64.2 0.9 slice_reduce_fusion
  65.7 0.9 fusion.23
  66.6 1.0 bitcast_select_fusion.2.q_heads
  67.7 1.6 fusion.2
  70.0 28.9 %all-gather.8.cloned.1.call-done.kv = bf16[8192,384]{1,0:T(8,128)(2,1)} async-done(((bf16[512,384]{1,0:T(8,128)(2,1)}), bf16[8192,384]{1,0:T(8,128)(2,1)}) %all-gather.8.cloned.1.call-update) | async-done | bytes 6291472 | tf_op jit(solution)/shard_map/all_gather | solution.py:727
  99.1 15.6 %attend.1 = (bf16[192,512]{1,0:T(8,128)(2,1)}, f32[512,256]{1,0:T(8,128)}, f32[2,768,1]{2,1,0:T(8,128)}) custom-call(s32[32]{0:T(128)} %select_reduce_fusion.slots, s32[2]{0:T(128)} %fusion.21.own, bf16[2,768,256]{2,1,0:T(8,128)(2,1)} %bitcast_select_fusion.2.q_heads, bf16[8192,384]{1,0:T(8,128)(2,1)} %all-gather.8.cloned.1.call-done.kv), custom_call_target="tpu_custom_call" | custom-call | flops 12884901888 | bytes 6291456 | tf_op jit(solution)/shard_map/attend/pallas_call | solution.py:393
  114.7 1.0 broadcast_in_dim.198
  115.7 16.9 %all_to_all.35 = bf16[4,192,512]{2,1,0:T(8,128)(2,1)} all-to-all(bf16[4,192,512]{2,1,0:T(8,128)(2,1)S(1)} %broadcast_in_dim.198), channel_id=1, replica_groups=mesh['batch'=2,'xlo'=2,'z'=4,'core'=2,'ulysses'=4] {'ulysses'}, dimensions={0} | all-to-all | bytes 1572864 | tf_op jit(solution)/shard_map/all_to_all | solution.py:612
  132.8 15.1 %all-gather.10.cloned.1.call-done.w_up.w_out.w_down = bf16[768,2304]{1,0:T(8,128)(2,1)} async-done(((bf16[24,2304]{1,0:T(8,128)(2,1)}), bf16[768,2304]{1,0:T(8,128)(2,1)}) %all-gather.10.cloned.1.call-update) | async-done | bytes 3538960 | tf_op jit(solution)/shard_map/all_gather | solution.py:741
  147.9 10.5 %feed_forward.1 = (f32[128,768]{1,0:T(8,128)}, bf16[512,768]{1,0:T(8,128)(2,1)}, bf16[512,768]{1,0:T(8,128)(2,1)}, bf16[512,768]{1,0:T(8,128)(2,1)}, bf16[512,768]{1,0:T(8,128)(2,1)}, /*index=5*/bf16[512,768]{1,0:T(8,128)(2,1)}) custom-call(s32[1]{0:T(128)} %bitcast.1.me, bf16[512,1536]{1,0:T(8,128)(2,1)} %all-gather.6.cloned.1.call-done.x.df, ...), custom_call_target="tpu_custom_call" | custom-call | flops 3019898880 | bytes 3538944 | tf_op jit(solution)/shard_map/feed_forward/pallas_call | solution.py:490
  158.5 4.4 %all-to-all-start.2 = ((bf16[4,128,768]{2,1,0:T(8,128)(2,1)}), bf16[4,128,768]{2,1,0:T(8,128)(2,1)S(1)}, u32[]{:S(2)}, u32[]{:S(2)}) async-start(bf16[4,128,768]{2,1,0:T(8,128)(2,1)} %bitcast.76), calls=%async_computation.2 | async-start | bytes 1572864 | tf_op jit(solution)/shard_map/all_to_all | solution.py:618
  164.3 11.3 %all-to-all-done.2 = bf16[4,128,768]{2,1,0:T(8,128)(2,1)S(1)} async-done(((bf16[4,128,768]{2,1,0:T(8,128)(2,1)}), bf16[4,128,768]{2,1,0:T(8,128)(2,1)S(1)}, u32[]{:S(2)}, u32[]{:S(2)}) %all-to-all-start.2) | async-done | bytes 786464 | tf_op jit(solution)/shard_map/all_to_all | solution.py:618
  176.2 0.9 convert_reduce_fusion.7
  177.1 0.9 broadcast_in_dim.199
  178.1 3.5 %all-to-all-start.3 = ((bf16[4,128,768]{2,1,0:T(8,128)(2,1)}), bf16[4,128,768]{2,1,0:T(8,128)(2,1)S(1)}, u32[]{:S(2)}, u32[]{:S(2)}) async-start(bf16[4,128,768]{2,1,0:T(8,128)(2,1)} %broadcast_in_dim.199), calls=%async_computation.3 | async-start | bytes 1572864 | tf_op jit(solution)/shard_map/all_to_all | solution.py:612
  183.1 1.0 constant_dynamic-slice_fusion.3
  186.2 7.2 %all-to-all-done.3 = bf16[4,128,768]{2,1,0:T(8,128)(2,1)S(1)} async-done(((bf16[4,128,768]{2,1,0:T(8,128)(2,1)}), bf16[4,128,768]{2,1,0:T(8,128)(2,1)S(1)}, u32[]{:S(2)}, u32[]{:S(2)}) %all-to-all-start.3) | async-done | bytes 786464 | tf_op jit(solution)/shard_map/all_to_all | solution.py:612
  193.4 0.9 copy-done.2
  194.3 4.4 %prepare.1 = (bf16[512,256]{1,0:T(8,128)(2,1)}, bf16[2,768,256]{2,1,0:T(8,128)(2,1)}, bf16[2,768,256]{2,1,0:T(8,128)(2,1)}) custom-call(bf16[512,768]{1,0:T(8,128)(2,1)} %bitcast.67, bf16[256,768]{1,0:T(8,128)(2,1)} %pad.38.w_out, f32[512,256]{1,0:T(8,128)} %get-tuple-element.90.ctx, f32[2,768,1]{2,1,0:T(8,128)} %get-tuple-element.91.lse, ...), custom_call_target="tpu_custom_call" | custom-call | flops 201326592 | bytes 1572864 | tf_op jit(solution)/shard_map/prepare/pallas_call | solution.py:393
  198.7 6.1 %weight_grads.1 = (f32[16,56,768]{2,1,0:T(8,128)}, bf16[16,56,768]{2,1,0:T(8,128)(2,1)}) custom-call(s32[1]{0:T(128)} %bitcast.core, bf16[512,768]{1,0:T(8,128)(2,1)} %get-tuple-element.80.h2, bf16[512,768]{1,0:T(8,128)(2,1)} %get-tuple-element.81.du, bf16[512,768]{1,0:T(8,128)(2,1)} %get-tuple-element.82.act, ...), custom_call_target="tpu_custom_call" | custom-call | flops 1207959552 | bytes 3538944 | tf_op jit(solution)/shard_map/weight_grads/pallas_call | solution.py:547
  204.9 3.2 collective-permute-done
  208.2 3.2 add_convert_fusion
  211.4 18.3 %query_grad.1.d_query = bf16[512,256]{1,0:T(8,128)(2,1)} custom-call(s32[32]{0:T(128)} %select_reduce_fusion.slots, s32[2]{0:T(128)} %fusion.21.own, bf16[2,768,256]{2,1,0:T(8,128)(2,1)} %get-tuple-element.95.q_ext, bf16[2,768,256]{2,1,0:T(8,128)(2,1)} %get-tuple-element.96.d_ext, bf16[8192,384]{1,0:T(8,128)(2,1)} %all-gather.8.cloned.1.call-done.kv), custom_call_target="tpu_custom_call" | custom-call | flops 19327352832 | bytes 6291456 | tf_op jit(solution)/shard_map/query_grad/pallas_call | solution.py:393
  229.6 4.1 %all-gather.14.cloned.1.call-done.p_all = bf16[8192,256]{1,0:T(8,128)(2,1)} async-done(((bf16[512,256]{1,0:T(8,128)(2,1)}), bf16[8192,256]{1,0:T(8,128)(2,1)}) %all-gather.14.cloned.1.call-update) | async-done | bytes 4194320 | tf_op jit(solution)/shard_map/all_gather | solution.py:789
  233.7 8.5 %all-to-all-start.4 = ((bf16[16,56,768]{2,1,0:T(8,128)(2,1)}), bf16[16,56,768]{2,1,0:T(8,128)(2,1)S(1)}, u32[]{:S(2)}, u32[]{:S(2)}) async-start(bf16[16,56,768]{2,1,0:T(8,128)(2,1)} %add_convert_fusion), calls=%async_computation.4 | async-start | bytes 2752512 | tf_op jit(solution)/shard_map/all_to_all | solution.py:796
  242.2 20.1 %key_grad.1 = (bf16[512,256]{1,0:T(8,128)(2,1)}, bf16[512,192]{1,0:T(8,128)(2,1)}) custom-call(s32[32]{0:T(128)} %select_reduce_fusion.slots, s32[2]{0:T(128)} %fusion.21.own, bf16[2,768,256]{2,1,0:T(8,128)(2,1)} %get-tuple-element.98.k_heads, bf16[2,768,256]{2,1,0:T(8,128)(2,1)} %get-tuple-element.99.v_heads, ...), custom_call_target="tpu_custom_call" | custom-call | flops 25769803776 | bytes 6291456 | tf_op jit(solution)/shard_map/key_grad/pallas_call | solution.py:393
  262.3 5.3 %finish.1 = (bf16[512,768]{1,0:T(8,128)(2,1)}, f32[16,32,640]{2,1,0:T(8,128)}, bf16[16,32,640]{2,1,0:T(8,128)(2,1)}) custom-call(s32[1]{0:T(128)} %bitcast.core, s32[1]{0:T(128)} %bitcast.1.me, bf16[512,256]{1,0:T(8,128)(2,1)} %query_grad.1.d_query, bf16[512,256]{1,0:T(8,128)(2,1)} %get-tuple-element.102.d_key, bf16[512,192]{1,0:T(8,128)(2,1)} %get-tuple-element.105.d_value, ...), custom_call_target="tpu_custom_call" | custom-call | flops 1006632960 | bytes 2949120 | tf_op jit(solution)/shard_map/finish/pallas_call | solution.py:393
  268.7 1.4 collective-permute-done.1
  270.2 1.0 dynamic-slice_bitcast_fusion.2
  271.8 2.9 collective-permute-start.3
  274.7 1.5 collective-permute-start.4
  278.1 1.4 broadcast_in_dim.201
  279.4 2.1 add_convert_fusion.1
  281.5 15.1 %all-to-all-start.5 = ((bf16[16,32,640]{2,1,0:T(8,128)(2,1)}), bf16[16,32,640]{2,1,0:T(8,128)(2,1)}, u32[]{:S(2)}, u32[]{:S(2)}) async-start(bf16[16,32,640]{2,1,0:T(8,128)(2,1)} %add_convert_fusion.1), calls=%async_computation.5 | async-start | bytes 1310720 | tf_op jit(solution)/shard_map/all_to_all | solution.py:810
  296.6 1.4 fusion.1
  298.3 10.7 %all-to-all-done.5 = bf16[16,32,640]{2,1,0:T(8,128)(2,1)} async-done(((bf16[16,32,640]{2,1,0:T(8,128)(2,1)}), bf16[16,32,640]{2,1,0:T(8,128)(2,1)}, u32[]{:S(2)}, u32[]{:S(2)}) %all-to-all-start.5) | async-done | bytes 655392 | tf_op jit(solution)/shard_map/all_to_all | solution.py:810
  309.0 1.2 convert_reduce_fusion.4
  311.0 4.2 %all-to-all-start.6 = ((f32[4,6,1408]{2,1,0:T(8,128)}), f32[4,6,1408]{2,1,0:T(8,128)S(1)}, u32[]{:S(2)}, u32[]{:S(2)}) async-start(f32[4,6,1408]{2,1,0:T(8,128)} %concatenate.51), calls=%async_computation.6 | async-start | bytes 360448 | tf_op jit(solution)/shard_map/all_to_all | solution.py:824
  315.2 1.1 fusion.11
  316.3 5.2 %all-to-all-done.6 = f32[4,6,1408]{2,1,0:T(8,128)S(1)} async-done(((f32[4,6,1408]{2,1,0:T(8,128)}), f32[4,6,1408]{2,1,0:T(8,128)S(1)}, u32[]{:S(2)}, u32[]{:S(2)}) %all-to-all-start.6) | async-done | bytes 135200 | tf_op jit(solution)/shard_map/all_to_all | solution.py:824
  323.3 1.1 reshape.317
  (180 shorter events, 25.9 us)
Async XLA Ops:
  7.2 6.9 %copy-start.3 = (bf16[128,768]{1,0:T(8,128)(2,1)S(1)}, bf16[128,768]{1,0:T(8,128)(2,1)}, u32[]{:S(2)}) copy-start(bf16[128,768]{1,0:T(8,128)(2,1)} %param.13) | copy-start | bytes 589828
  7.2 6.9 %copy-start.6 = (f32[128,768]{1,0:T(8,128)S(1)}, f32[128,768]{1,0:T(8,128)}, u32[]{:S(2)}) copy-start(f32[128,768]{1,0:T(8,128)} %param.25) | copy-start | bytes 1179652
  7.2 47.8 %all-gather.6.cloned.1.call-start = ((), (), s32[]{:S(2)}) async-start(), calls=%async_computation.7 | async-start | bytes 1966080 | tf_op jit(solution)/shard_map/all_gather | solution.py:702
  15.6 10.6 %all-to-all-start = ((bf16[4,24,768]{2,1,0:T(8,128)(2,1)}), bf16[4,24,768]{2,1,0:T(8,128)(2,1)S(1)}, u32[]{:S(2)}, u32[]{:S(2)}) async-start(bf16[4,24,768]{2,1,0:T(8,128)(2,1)} %copy.86), calls=%async_computation | async-start | bytes 294912 | tf_op jit(solution)/shard_map/all_to_all | solution.py:700
  20.1 78.7 %all-gather.8.cloned.1.call-start = ((), (), s32[]{:S(2)}) async-start(), calls=%async_computation.8 | async-start | bytes 6684672 | tf_op jit(solution)/shard_map/all_gather | solution.py:727
  55.0 4.0 %copy-start.19 = (s32[1,32]{1,0:T(1,128)S(1)}, s32[1,32]{1,0:T(1,128)}, u32[]{:S(2)}) copy-start(s32[1,32]{1,0:T(1,128)} %param.14) | copy-start | bytes 388
  55.0 5.5 %copy-start.15 = (bf16[1,24,768]{2,1,0:T(8,128)(2,1)S(1)}, bf16[1,24,768]{2,1,0:T(8,128)(2,1)}, u32[]{:S(2)}) copy-start(bf16[1,24,768]{2,1,0:T(8,128)(2,1)} %param.23) | copy-start | bytes 110596
  58.8 6.4 %copy-start.5 = (bf16[512,384]{1,0:T(8,128)(2,1)S(1)}, bf16[512,384]{1,0:T(8,128)(2,1)}, u32[]{:S(2)}) copy-start(bf16[512,384]{1,0:T(8,128)(2,1)} %get-tuple-element.67) | copy-start | bytes 1179652
  58.8 89.1 %all-gather.10.cloned.1.call-start = ((), (), s32[]{:S(2)}) async-start(), calls=%async_computation.9 | async-start | bytes 3649536 | tf_op jit(solution)/shard_map/all_gather | solution.py:741
  60.5 5.1 %copy-start.13 = (bf16[512,192]{1,0:T(8,128)(2,1)S(1)}, bf16[512,192]{1,0:T(8,128)(2,1)}, u32[]{:S(2)}) copy-start(bf16[512,192]{1,0:T(8,128)(2,1)} %get-tuple-element.68) | copy-start | bytes 589828
  98.9 94.5 %all-gather.12.cloned.1.call-start = ((), (), s32[]{:S(2)}) async-start(), calls=%async_computation.10 | async-start | bytes 4456448 | tf_op jit(solution)/shard_map/all_gather | solution.py:746
  158.5 5.2 %copy-start.1 = (bf16[4,192,512]{2,1,0:T(8,128)(2,1)S(1)}, bf16[4,192,512]{2,1,0:T(8,128)(2,1)}, u32[]{:S(2)}) copy-start(bf16[4,192,512]{2,1,0:T(8,128)(2,1)} %all_to_all.35) | copy-start | bytes 2359300
  158.5 5.5 %copy-start = (f32[128,768]{1,0:T(8,128)S(1)}, f32[128,768]{1,0:T(8,128)}, u32[]{:S(2)}) copy-start(f32[128,768]{1,0:T(8,128)} %get-tuple-element.83) | copy-start | bytes 1179652
  158.5 17.1 %all-to-all-start.2 = ((bf16[4,128,768]{2,1,0:T(8,128)(2,1)}), bf16[4,128,768]{2,1,0:T(8,128)(2,1)S(1)}, u32[]{:S(2)}, u32[]{:S(2)}) async-start(bf16[4,128,768]{2,1,0:T(8,128)(2,1)} %bitcast.76), calls=%async_computation.2 | async-start | bytes 1572864 | tf_op jit(solution)/shard_map/all_to_all | solution.py:618
  164.0 12.2 %copy-start.7 = (f32[128,768]{1,0:T(8,128)S(1)}, f32[128,768]{1,0:T(8,128)}, u32[]{:S(2)}) copy-start(f32[128,768]{1,0:T(8,128)} %param.25) | copy-start | bytes 1179652
  177.1 5.5 %copy-start.4 = (bf16[512,768]{1,0:T(8,128)(2,1)S(1)}, bf16[512,768]{1,0:T(8,128)(2,1)}, u32[]{:S(2)}) copy-start(bf16[512,768]{1,0:T(8,128)(2,1)} %get-tuple-element.81.du) | copy-start | bytes 2359300
  178.1 15.3 %all-to-all-start.3 = ((bf16[4,128,768]{2,1,0:T(8,128)(2,1)}), bf16[4,128,768]{2,1,0:T(8,128)(2,1)S(1)}, u32[]{:S(2)}, u32[]{:S(2)}) async-start(bf16[4,128,768]{2,1,0:T(8,128)(2,1)} %broadcast_in_dim.199), calls=%async_computation.3 | async-start | bytes 1572864 | tf_op jit(solution)/shard_map/all_to_all | solution.py:612
  181.6 52.2 %all-gather.14.cloned.1.call-start = ((), (), s32[]{:S(2)}) async-start(), calls=%async_computation.11 | async-start | bytes 4456448 | tf_op jit(solution)/shard_map/all_gather | solution.py:789
  193.4 0.9 copy-start.2
  204.8 3.3 %collective-permute-start = (bf16[16,56,768]{2,1,0:T(8,128)(2,1)}, bf16[16,56,768]{2,1,0:T(8,128)(2,1)S(1)}, u32[]{:S(2)}, u32[]{:S(2)}) collective-permute-start(bf16[16,56,768]{2,1,0:T(8,128)(2,1)} %get-tuple-element.89), channel_id=1, source_target_pairs={{0,4},{4,0},{1,5},{5,1},{2,6},{6,2},{3,7},{7,3},{8,12},{12,8},{9,1... | collective-permute-start | bytes 4128776 | tf_op jit(solution)/shard_map/ppermute | solution.py:623
  233.7 28.6 %all-to-all-start.4 = ((bf16[16,56,768]{2,1,0:T(8,128)(2,1)}), bf16[16,56,768]{2,1,0:T(8,128)(2,1)S(1)}, u32[]{:S(2)}, u32[]{:S(2)}) async-start(bf16[16,56,768]{2,1,0:T(8,128)(2,1)} %add_convert_fusion), calls=%async_computation.4 | async-start | bytes 2752512 | tf_op jit(solution)/shard_map/all_to_all | solution.py:796
  262.3 6.1 %copy-start.14 = (f32[128,6]{1,0:T(8,128)S(1)}, f32[128,6]{1,0:T(8,128)}, u32[]{:S(2)}) copy-start(f32[128,6]{1,0:T(8,128)} %get-tuple-element.171) | copy-start | bytes 9220
  267.6 2.4 copy-start.10
  267.6 2.4 collective-permute-start.1
  267.7 2.4 copy-start.16
  268.5 1.6 copy-start.11
  270.2 9.2 %copy-start.9 = (f32[16,32,640]{2,1,0:T(8,128)S(1)}, f32[16,32,640]{2,1,0:T(8,128)}, u32[]{:S(2)}) copy-start(f32[16,32,640]{2,1,0:T(8,128)} %get-tuple-element.113) | copy-start | bytes 3932164
  271.3 25.3 %collective-permute-start.2 = (bf16[128,1536]{1,0:T(8,128)(2,1)}, bf16[128,1536]{1,0:T(8,128)(2,1)}, u32[]{:S(2)}, u32[]{:S(2)}) collective-permute-start(bf16[128,1536]{1,0:T(8,128)(2,1)} %get-tuple-element.180), channel_id=1, source_target_pairs={{0,1},{1,2},{2,3},{3,0},{4,5},{5,6},{6,7},{7,4},{8,9},{9,10},{10,1... | collective-permute-start | bytes 1179656 | tf_op jit(solution)/shard_map/ppermute | solution.py:634
  271.8 24.8 %collective-permute-start.3 = (bf16[128,1536]{1,0:T(8,128)(2,1)}, bf16[128,1536]{1,0:T(8,128)(2,1)}, u32[]{:S(2)}, u32[]{:S(2)}) collective-permute-start(bf16[128,1536]{1,0:T(8,128)(2,1)} %get-tuple-element.182), channel_id=1, source_target_pairs={{0,2},{1,3},{2,0},{3,1},{4,6},{5,7},{6,4},{7,5},{8,10},{9,11},{10,... | collective-permute-start | bytes 1179656 | tf_op jit(solution)/shard_map/ppermute | solution.py:634
  274.7 21.9 %collective-permute-start.4 = (bf16[128,1536]{1,0:T(8,128)(2,1)}, bf16[128,1536]{1,0:T(8,128)(2,1)}, u32[]{:S(2)}, u32[]{:S(2)}) collective-permute-start(bf16[128,1536]{1,0:T(8,128)(2,1)} %get-tuple-element.181), channel_id=1, source_target_pairs={{0,3},{1,0},{2,1},{3,2},{4,7},{5,4},{6,5},{7,6},{8,11},{9,8},{10,9... | collective-permute-start | bytes 1179656 | tf_op jit(solution)/shard_map/ppermute | solution.py:634
  281.5 16.6 %copy-start.17 = (f32[128]{0:T(128)S(1)}, f32[128]{0:T(128)}, u32[]{:S(2)}) copy-start(f32[128]{0:T(128)} %copy-done.16) | copy-start | bytes 1540
  281.5 16.6 %copy-start.18 = (f32[128]{0:T(128)S(1)}, f32[128]{0:T(128)}, u32[]{:S(2)}) copy-start(f32[128]{0:T(128)} %add_rsqrt_fusion) | copy-start | bytes 1540
  281.5 27.5 %all-to-all-start.5 = ((bf16[16,32,640]{2,1,0:T(8,128)(2,1)}), bf16[16,32,640]{2,1,0:T(8,128)(2,1)}, u32[]{:S(2)}, u32[]{:S(2)}) async-start(bf16[16,32,640]{2,1,0:T(8,128)(2,1)} %add_convert_fusion.1), calls=%async_computation.5 | async-start | bytes 1310720 | tf_op jit(solution)/shard_map/all_to_all | solution.py:810
  296.6 13.7 %copy-start.12 = (f32[4,6,768]{2,1,0:T(8,128)S(1)}, f32[4,6,768]{2,1,0:T(8,128)}, u32[]{:S(2)}) copy-start(f32[4,6,768]{2,1,0:T(8,128)} %reshape.309) | copy-start | bytes 221188
  298.0 17.2 %copy-start.8 = (f32[128,768]{1,0:T(8,128)S(1)}, f32[128,768]{1,0:T(8,128)}, u32[]{:S(2)}) copy-start(f32[128,768]{1,0:T(8,128)} %get-tuple-element.177) | copy-start | bytes 1179652
  311.0 10.4 %all-to-all-start.6 = ((f32[4,6,1408]{2,1,0:T(8,128)}), f32[4,6,1408]{2,1,0:T(8,128)S(1)}, u32[]{:S(2)}, u32[]{:S(2)}) async-start(f32[4,6,1408]{2,1,0:T(8,128)} %concatenate.51), calls=%async_computation.6 | async-start | bytes 360448 | tf_op jit(solution)/shard_map/all_to_all | solution.py:824
Sparse Core Ops, SparseCore 0:
  15.0 28.9 all-gather.5
  59.0 39.8 all-gather.7
  101.2 46.6 all-gather.9
  149.5 36.7 all-gather.11
  198.8 34.8 all-gather.13
where the time goes:
time: 340 us; the launch traced here: 333 us
  waiting for transfers between devices  93.2 us (27%)
  Pallas kernels  84.1 us (25%)
  starting transfers between devices  45.7 us (13%)
  blocking collectives  45.4 us (13%)
  local copies, waits for them, and re-layouts  29.3 us (9%)
  other arithmetic  20.2 us (6%)
  between operations  14.9 us (4%)
    pallas_call x5, Pallas kernels, call(): pl.pallas_call(functools.partial(kernel, **static), out_shape=tuple((jax....  63.7 us
    all_gather x1, waiting for transfers between devices, on_device(): kv_all = lax.all_gather(kv, BLK, axis=0, tiled=True)  28.9 us
    all_gather x1, blocking collectives, on_device(): filled = lax.all_gather(piece, WIDE, axis=0, tiled=True)  28.5 us
    all_to_all x1, blocking collectives, to_all(): return lax.all_to_all(sent, axis, split_axis=0, concat_axis=0, tiled=True)  16.9 us
    all_gather x1, waiting for transfers between devices, on_device(): ffn_all = lax.all_gather(ffn, WIDE, axis=0, tiled=True)  15.1 us
    all_to_all x1, starting transfers between devices, on_device(): late = lax.all_to_all(late, CHIPS, split_axis=0, concat_axis=0, tiled=True)  15.1 us
    all_to_all x1, waiting for transfers between devices, summed_at_owner(): got = lax.all_to_all(sent, axis, split_axis=0, concat_axis=0, tiled=True)  11.3 us
    all_to_all x1, waiting for transfers between devices, on_device(): late = lax.all_to_all(late, CHIPS, split_axis=0, concat_axis=0, tiled=True)  10.7 us
  transfers between devices with their start and end apart: 16, of which 10 were waited for; matrix products, arithmetic and copies ran while one was open for 10% of the time, Pallas kernels for 21%

commit v1 on v0

--- a/solution.py
+++ b/solution.py
@@ -12,7 +12,7 @@
 HEAD_DIM = 64
 NORM_EPS = 1e-05
 FLOOR = -1e25
-HIGHEST_ABOVE = 60.0
+LARGEST_SUM = 1e25
 LANES = 256
 EXTRA = 64
 BELOW_FLOOR = -1e30
@@ -98,7 +98,7 @@
 
 
 def attend_kernel(
-    slots, own, q_heads, kv, ctx_low, ctx, lse, shift, total, q_ext, top, *, half, heads
+    slots, own, q_heads, kv, ctx_low, ctx, lse, shift, total, q_ext, *, half, heads
 ):
     deep = heads * half
     lane = lanes_of(deep)
@@ -113,27 +113,24 @@
         q_ext[...] = jnp.where(lane == heads * HEAD_DIM, -first, q_heads[part].astype(F32)).astype(
             BF16
         )
-        top[...] = jnp.zeros_like(top)
         total[...] = mm(jnp.exp(scores - first).astype(BF16), ones_before(kv[here, 128:]))
 
         def tiles(ranks):
             at = [stretch(slots[r], half) for r in ranks]
-            added = [total[...], top[...]]
+            added = [total[...]]
 
             def produce(a):
                 return mm_nt(q_ext[...], ones_after(kv[a, :LANES], heads * HEAD_DIM))
 
             def consume(a, above):
-                added[1] = jnp.maximum(added[1], jnp.max(above.reshape(deep // 8, 8, half), axis=0))
                 added[0] += mm(jnp.exp(above).astype(BF16), ones_before(kv[a, 128:]))
 
             one_ahead(at, produce, consume)
             total[...] = added[0]
-            top[...] = added[1]
 
         in_groups(0, rank_own, tiles)
 
-        @pl.when(jnp.logical_not(jnp.max(top[...]) < HIGHEST_ABOVE))
+        @pl.when(jnp.logical_not(jnp.max(total[:, :EXTRA]) < LARGEST_SUM))
         def _():
             shift[...] = jnp.full_like(shift, FLOOR)
             total[...] = jnp.zeros_like(total)
@@ -162,10 +159,29 @@
     lax.fori_loop(0, 2, one_half, 0)
 
 
-def query_grad_kernel(slots, own, q_ext, d_ext, kv, d_query, total, *, half, heads):
+def query_grad_kernel(
+    slots, own, q_heads, packed, kv, d_query, total, q_ext, d_ext, *, half, heads
+):
+    lane = lanes_of(half)
+
     def one_half(part, _):
         rank_own = own[part]
         total[...] = jnp.zeros_like(total)
+        grads = packed[stretch(part, half), :].astype(F32)
+        for h in range(heads):
+            deep = slice(h * half, (h + 1) * half)
+            first = EXTRA + h * HEAD_DIM
+            q_new = q_heads[part, deep, :].astype(F32)
+            d_new = jnp.where(
+                jnp.logical_and(lane >= first, lane < first + HEAD_DIM), grads, 0.0
+            )
+            for i in range(3):
+                at = 3 * h + i
+                q_new = jnp.where(lane == heads * HEAD_DIM + i, grads[:, at : at + 1], q_new)
+                at += 3 * heads
+                d_new = jnp.where(lane == i, grads[:, at : at + 1], d_new)
+            q_ext[deep, :] = q_new.astype(BF16)
+            d_ext[deep, :] = d_new.astype(BF16)
 
         def tiles(ranks, mask=None):
             at = [stretch(slots[r], half) for r in ranks]
@@ -173,8 +189,8 @@
 
             def produce(a):
                 return (
-                    mm_nt(q_ext[part], ones_after(kv[a, :LANES], heads * HEAD_DIM)),
-                    mm_nt(d_ext[part], ones_before(kv[a, 128:])),
+                    mm_nt(q_ext[...], ones_after(kv[a, :LANES], heads * HEAD_DIM)),
+                    mm_nt(d_ext[...], ones_before(kv[a, 128:])),
                 )
 
             def consume(a, ready):
@@ -236,31 +252,23 @@
     lax.fori_loop(0, 2, one_half, 0)
 
 
-def prepare_kernel(dc, w_out, ctx, lse, q_heads, packed, q_ext, d_ext, *, half, heads):
+def prepare_kernel(dc, w_out, ctx, lse, packed, *, half, heads):
     lane = lanes_of(half)
-    d_ctx = mm_nt(dc[...], w_out[...]).astype(BF16)
+    d_ctx = mm_nt(dc[...], w_out[...]).astype(BF16).astype(F32)
     for part in range(2):
         rows = slice(part * half, (part + 1) * half)
         grads = d_ctx[rows, :]
-        terms = grads.astype(F32) * ctx[rows, :]
-        extra = grads.astype(F32)
+        terms = grads * ctx[rows, :]
         for h in range(heads):
-            deep = slice(h * half, (h + 1) * half)
             first = EXTRA + h * HEAD_DIM
             here = jnp.logical_and(lane >= first, lane < first + HEAD_DIM)
             delta = jnp.sum(jnp.where(here, terms, 0.0), axis=1, keepdims=True)
-            minus_lse = three(-lse[part, deep, :])
+            minus_lse = three(-lse[part, h * half : (h + 1) * half, :])
             minus_delta = three(-delta)
-            q_new = q_heads[part, deep, :].astype(F32)
-            d_new = jnp.where(here, grads.astype(F32), 0.0)
             for i in range(3):
-                q_new = jnp.where(lane == heads * HEAD_DIM + i, minus_lse[i], q_new)
-                d_new = jnp.where(lane == i, minus_delta[i], d_new)
-                extra = jnp.where(lane == 3 * h + i, minus_lse[i], extra)
-                extra = jnp.where(lane == 3 * (heads + h) + i, minus_delta[i], extra)
-            q_ext[part, deep, :] = q_new.astype(BF16)
-            d_ext[part, deep, :] = d_new.astype(BF16)
-        packed[rows, :] = extra.astype(BF16)
+                grads = jnp.where(lane == 3 * h + i, minus_lse[i], grads)
+                grads = jnp.where(lane == 3 * (heads + h) + i, minus_delta[i], grads)
+        packed[rows, :] = grads.astype(BF16)
 
 
 def project_kernel(me, x, weights, h1, n1, kv, q, vec, bias, *, wide, ways, pair, part):
@@ -413,28 +421,28 @@
     return call(
         attend_kernel, "attend", (slots, own), (q_heads, kv),
         [((width, 2 * half), BF16), ((2 * half, LANES), F32), ((2, deep, 1), F32)],
-        [((deep, 1), F32), ((deep, LANES), F32), ((deep, LANES), BF16), ((8, half), F32)],
+        [((deep, 1), F32), ((deep, LANES), F32), ((deep, LANES), BF16)],
         cost(2 * half, kv.shape[0], heads, 2), half=half, heads=heads,
     )
 
 
-def prepare(dc, w_out, ctx, lse, q_heads, heads):
+def prepare(dc, w_out, ctx, lse, heads):
+    half = dc.shape[0] // 2
+    return call(
+        prepare_kernel, "prepare", (), (dc, w_out, ctx, lse),
+        [((2 * half, LANES), BF16)], [],
+        pl.CostEstimate(flops=2 * dc.size * LANES, bytes_accessed=8 * ctx.size, transcendentals=0),
+        half=half, heads=heads,
+    )[0]
+
+
+def query_grad(slots, own, q_heads, packed, kv, heads):
     _, deep, _ = q_heads.shape
     half = deep // heads
     return call(
-        prepare_kernel, "prepare", (), (dc, w_out, ctx, lse, q_heads),
-        [((2 * half, LANES), BF16), (q_heads.shape, BF16), (q_heads.shape, BF16)], [],
-        pl.CostEstimate(flops=2 * dc.size * LANES, bytes_accessed=4 * q_heads.size, transcendentals=0),
-        half=half, heads=heads,
-    )
-
-
-def query_grad(slots, own, q_ext, d_ext, kv, heads):
-    _, deep, _ = q_ext.shape
-    half = deep // heads
-    return call(
-        query_grad_kernel, "query_grad", (slots, own), (q_ext, d_ext, kv),
-        [((2 * half, LANES), BF16)], [((deep, LANES), F32)],
+        query_grad_kernel, "query_grad", (slots, own), (q_heads, packed, kv),
+        [((2 * half, LANES), BF16)],
+        [((deep, LANES), F32), ((deep, LANES), BF16), ((deep, LANES), BF16)],
         cost(2 * half, kv.shape[0], heads, 3), half=half, heads=heads,
     )[0]
 
@@ -684,18 +692,14 @@
         axis=0,
     )
     qkv_slices = w_qkv[0].reshape(held, 3, ways, part).transpose(2, 0, 1, 3).reshape(ways, held, 3 * part)
-    up_slices = w_up[0].reshape(held, wide, ways, ff_held).transpose(2, 0, 1, 3).reshape(ways, held, ff_part)
-    first = jnp.concatenate(
+    sent = jnp.concatenate(
         [
             qkv_slices,
             jnp.broadcast_to(small[None], (ways,) + small.shape),
-            jnp.zeros((ways, held, width - 3 * part - pair), BF16),
+            jnp.zeros((ways, held, 64 - pair), BF16),
         ],
         axis=2,
     )
-    blank = jnp.zeros((ways, 8 - held, width), BF16)
-    wide_out = jnp.broadcast_to(w_out[0][None], (ways, held, width))
-    sent = jnp.concatenate([first, blank, up_slices, blank, wide_out, blank], axis=1)
     sent, tokens_late, cotangent_late = lax.optimization_barrier((sent, tokens, cotangent))
     got = lax.all_to_all(sent, "ulysses", split_axis=0, concat_axis=0, tiled=True)
     df_own = cotangent_late.astype(BF16)
@@ -707,14 +711,6 @@
     vector = jnp.pad(vector, ((0, (ways - 1) * held), (0, 64 - ways * pair)))
     piece = jnp.concatenate([matrix, vector], axis=1)
     filled = lax.all_gather(piece, WIDE, axis=0, tiled=True)
-    ffn = jnp.concatenate(
-        [
-            got[:, 8 : 8 + held].reshape(ways * held, width),
-            got[:, 16 : 16 + held].reshape(ways * held, width),
-            w_down[0],
-        ],
-        axis=1,
-    )
     h1, n1, kv, q_scaled, vec = project(me[None], both, filled, part, wide, ways, pair)
     gains, shifts = vec[0], vec[1]
     halves = vec[3].reshape(wide * ways, 2, held)
@@ -725,6 +721,12 @@
     )
     up_bias_u = up_bias_u.transpose(1, 0, 2).reshape(-1)
     kv_all = lax.all_gather(kv, BLK, axis=0, tiled=True)
+
+    up_late, out_late, kv = lax.optimization_barrier((w_up[0], w_out[0], kv))
+    up_slices = up_late.reshape(held, wide, ways, ff_held).transpose(2, 0, 1, 3).reshape(ways, held, ff_part)
+    sent = jnp.concatenate([up_slices, jnp.broadcast_to(out_late[None], (ways, held, width))], axis=2)
+    got = lax.all_to_all(sent, "ulysses", split_axis=0, concat_axis=0, tiled=True)
+    ffn = jnp.concatenate([got.reshape(ways * held, ff_part + width), w_down[0]], axis=1)
     q_heads = head_lanes(q_scaled, heads, 0)
     k_heads = head_lanes(kv[:, :part], heads, EXTRA, 0)
     v_heads = head_lanes(kv[:, part:], heads, EXTRA, 3 * heads)
@@ -785,13 +787,13 @@
     w_out_u = lax.dynamic_slice(ffn_all, (me * part, width), (part, width))
 
     w_out_wide = jnp.pad(w_out_u, ((EXTRA, 0), (0, 0)))
-    packed, q_ext, d_ext = prepare(dc, w_out_wide, ctx, lse, q_heads, heads)
+    packed = prepare(dc, w_out_wide, ctx, lse, heads)
     packed_all = lax.all_gather(packed, BLK, axis=0, tiled=True)
     core = lax.axis_index("core")
     early, early_sent = weight_grads(core[None], h2, du, act, both, ctx_rows, dc, wide)
     early = (early + other_core(early_sent).astype(F32)).astype(BF16)
-    early, q_ext = lax.optimization_barrier((early, q_ext))
-    d_query = query_grad(slots, own, q_ext, d_ext, kv_all, heads)
+    early, q_heads = lax.optimization_barrier((early, q_heads))
+    d_query = query_grad(slots, own, q_heads, packed, kv_all, heads)
     early, packed_all, d_query = lax.optimization_barrier((early, packed_all, d_query))
     early = lax.all_to_all(early, CHIPS, split_axis=0, concat_axis=0, tiled=True)
     d_key, d_value = key_grad(slots, own, k_heads, v_heads, q_all, packed_all, heads)
@@ -800,15 +802,15 @@
     terms, late, late_sent = finish(
         core[None], me[None], d_query, d_key, d_value, h1, n1, filled, small_grads
     )
-    terms, late_got = lax.optimization_barrier((terms, other_core(late_sent)))
+    late = (late + other_core(late_sent).astype(F32)).astype(BF16)
+    terms, late = lax.optimization_barrier((terms, late))
+    late = lax.all_to_all(late, CHIPS, split_axis=0, concat_axis=0, tiled=True)
+    late = jnp.sum(late.astype(F32), axis=0)
     pair_sums = reduced(
         jnp.concatenate([terms, down], axis=1).reshape(ways, own_rows, 2 * width), "ulysses"
     )
     dh1 = pair_sums[:, :width]
     result = pair_sums[:, width:] + x2_own + down_bias_all
-    late = (late + late_got.astype(F32)).astype(BF16)
-    late = lax.all_to_all(late, CHIPS, split_axis=0, concat_axis=0, tiled=True)
-    late = jnp.sum(late.astype(F32), axis=0)
     n1_own, r1_own = normalized(tokens.astype(F32))
     d_tokens = dx2 + norm_back(dh1, gains[:width], n1_own, r1_own)
 

time: 340 us -> 338 us (level)
  the two profiles are of different devices: /device:TPU:0 before, /device:TPU:4 now
where the time goes in v1:
time: 338 us; the launch traced here: 332 us
  waiting for transfers between devices  92.5 us (27%)
  Pallas kernels  84.3 us (25%)
  starting transfers between devices  50.3 us (15%)
  blocking collectives  41.8 us (12%)
  local copies, waits for them, and re-layouts  25.8 us (8%)
  other arithmetic  22.9 us (7%)
  between operations  14.8 us (4%)
    pallas_call x5, Pallas kernels, call(): pl.pallas_call(functools.partial(kernel, **static), out_shape=tuple((jax....  63.8 us
    all_gather x1, blocking collectives, on_device(): filled = lax.all_gather(piece, WIDE, axis=0, tiled=True)  28.1 us
    all_gather x1, waiting for transfers between devices, on_device(): kv_all = lax.all_gather(kv, BLK, axis=0, tiled=True)  24.1 us
    all_gather x1, waiting for transfers between devices, on_device(): ffn_all = lax.all_gather(ffn, WIDE, axis=0, tiled=True)  16.8 us
    all_to_all x1, blocking collectives, to_all(): return lax.all_to_all(sent, axis, split_axis=0, concat_axis=0, tiled=True)  13.7 us
    ppermute x2, starting transfers between devices, other_core(): return lax.ppermute(x, 'core', [(0, 1), (1, 0)])  13.5 us
    ppermute x3, waiting for transfers between devices, reduced(): lax.ppermute(rows_of(k).astype(BF16), axis, [(i, (i + k) % ways) for i in...  12.4 us
    all_to_all x1, waiting for transfers between devices, summed_at_owner(): got = lax.all_to_all(sent, axis, split_axis=0, concat_axis=0, tiled=True)  11.3 us
  transfers between devices with their start and end apart: 17, of which 13 were waited for; matrix products, arithmetic and copies ran while one was open for 9% of the time, Pallas kernels for 22%

profile of v1, /device:TPU:4, one launch (start us, length us, event | category | flops | bytes accessed | tf_op | source)
XLA Modules:
  0.0 332.4 jit_solution(13665990920439867078)
XLA Ops:
  8.7 1.3 reduce.18
  11.8 1.0 convert_reduce_fusion.6
  12.8 1.7 pad_maximum_fusion.1
  15.2 4.5 %all-to-all-start = ((bf16[4,6,640]{2,1,0:T(8,128)(2,1)}), bf16[4,6,640]{2,1,0:T(8,128)(2,1)S(1)}, u32[]{:S(2)}, u32[]{:S(2)}) async-start(bf16[4,6,640]{2,1,0:T(8,128)(2,1)} %copy.82), calls=%async_computation | async-start | bytes 81920 | tf_op jit(solution)/shard_map/all_to_all | solution.py:704
  19.6 5.5 %all-to-all-done = bf16[4,6,640]{2,1,0:T(8,128)(2,1)S(1)} async-done(((bf16[4,6,640]{2,1,0:T(8,128)(2,1)}), bf16[4,6,640]{2,1,0:T(8,128)(2,1)S(1)}, u32[]{:S(2)}, u32[]{:S(2)}) %all-to-all-start) | async-done | bytes 30752 | tf_op jit(solution)/shard_map/all_to_all | solution.py:704
  25.4 28.1 %all_gather.19.weights = bf16[768,640]{1,0:T(8,128)(2,1)} all-gather(bf16[24,640]{1,0:T(8,128)(2,1)S(1)} %fusion.16), channel_id=1, replica_groups=mesh['batch'=2,'xlo'=2,'z'=4,'core'=2,'ulysses'=4] {'batch','xlo','z','c..., dimensions={0}, use_global_device_ids=true | all-gather | bytes 1013760 | tf_op jit(solution)/shard_map/all_gather | solution.py:713
  53.5 3.8 %project.1 = (bf16[512,768]{1,0:T(8,128)(2,1)}, f32[512,768]{1,0:T(8,128)}, bf16[512,384]{1,0:T(8,128)(2,1)}, bf16[512,192]{1,0:T(8,128)(2,1)}, f32[8,1536]{1,0:T(8,128)}) custom-call(s32[1]{0:T(128)} %bitcast.1.me, bf16[512,1536]{1,0:T(8,128)(2,1)} %all-gather.6.cloned.1.call-done.x.df, bf16[768,640]{1,0:T(8,128)(2,1)} %all_gather.19.weights), custom_call_target="tpu_custom_call" | custom-call | flops 503316480 | bytes 3145728 | tf_op jit(solution)/shard_map/project/pallas_call | solution.py:308
  63.7 3.3 all-to-all-start.1
  69.2 1.0 bitcast_select_fusion.2.q_heads
  70.3 1.6 fusion.2
  71.9 0.9 all-to-all-done.1
  73.5 24.1 %all-gather.8.cloned.1.call-done.kv = bf16[8192,384]{1,0:T(8,128)(2,1)} async-done(((bf16[512,384]{1,0:T(8,128)(2,1)}), bf16[8192,384]{1,0:T(8,128)(2,1)}) %all-gather.8.cloned.1.call-update) | async-done | bytes 6291472 | tf_op jit(solution)/shard_map/all_gather | solution.py:723
  97.9 17.1 %attend.1 = (bf16[192,512]{1,0:T(8,128)(2,1)}, f32[512,256]{1,0:T(8,128)}, f32[2,768,1]{2,1,0:T(8,128)}) custom-call(s32[32]{0:T(128)} %select_reduce_fusion.slots, s32[2]{0:T(128)} %fusion.21.own, bf16[2,768,256]{2,1,0:T(8,128)(2,1)} %bitcast_select_fusion.2.q_heads, bf16[8192,384]{1,0:T(8,128)(2,1)} %all-gather.8.cloned.1.call-done.kv), custom_call_target="tpu_custom_call" | custom-call | flops 12884901888 | bytes 6291456 | tf_op jit(solution)/shard_map/attend/pallas_call | solution.py:401
  115.0 1.0 broadcast_in_dim.192
  116.0 13.7 %all_to_all.40 = bf16[4,192,512]{2,1,0:T(8,128)(2,1)} all-to-all(bf16[4,192,512]{2,1,0:T(8,128)(2,1)S(1)} %broadcast_in_dim.192), channel_id=1, replica_groups=mesh['batch'=2,'xlo'=2,'z'=4,'core'=2,'ulysses'=4] {'ulysses'}, dimensions={0} | all-to-all | bytes 1572864 | tf_op jit(solution)/shard_map/all_to_all | solution.py:620
  129.9 16.8 %all-gather.10.cloned.1.call-done.w_up.w_out.w_down = bf16[768,2304]{1,0:T(8,128)(2,1)} async-done(((bf16[24,2304]{1,0:T(8,128)(2,1)}), bf16[768,2304]{1,0:T(8,128)(2,1)}) %all-gather.10.cloned.1.call-update) | async-done | bytes 3538960 | tf_op jit(solution)/shard_map/all_gather | solution.py:743
  146.6 10.5 %feed_forward.1 = (f32[128,768]{1,0:T(8,128)}, bf16[512,768]{1,0:T(8,128)(2,1)}, bf16[512,768]{1,0:T(8,128)(2,1)}, bf16[512,768]{1,0:T(8,128)(2,1)}, bf16[512,768]{1,0:T(8,128)(2,1)}, /*index=5*/bf16[512,768]{1,0:T(8,128)(2,1)}) custom-call(s32[1]{0:T(128)} %bitcast.1.me, bf16[512,1536]{1,0:T(8,128)(2,1)} %all-gather.6.cloned.1.call-done.x.df, ...), custom_call_target="tpu_custom_call" | custom-call | flops 3019898880 | bytes 3538944 | tf_op jit(solution)/shard_map/feed_forward/pallas_call | solution.py:498
  157.2 4.4 %all-to-all-start.3 = ((bf16[4,128,768]{2,1,0:T(8,128)(2,1)}), bf16[4,128,768]{2,1,0:T(8,128)(2,1)S(1)}, u32[]{:S(2)}, u32[]{:S(2)}) async-start(bf16[4,128,768]{2,1,0:T(8,128)(2,1)} %bitcast.78), calls=%async_computation.3 | async-start | bytes 1572864 | tf_op jit(solution)/shard_map/all_to_all | solution.py:626
  163.0 11.3 %all-to-all-done.3 = bf16[4,128,768]{2,1,0:T(8,128)(2,1)S(1)} async-done(((bf16[4,128,768]{2,1,0:T(8,128)(2,1)}), bf16[4,128,768]{2,1,0:T(8,128)(2,1)S(1)}, u32[]{:S(2)}, u32[]{:S(2)}) %all-to-all-start.3) | async-done | bytes 786464 | tf_op jit(solution)/shard_map/all_to_all | solution.py:626
  174.9 0.9 convert_reduce_fusion.7
  175.8 0.9 broadcast_in_dim.193
  176.8 3.5 %all-to-all-start.4 = ((bf16[4,128,768]{2,1,0:T(8,128)(2,1)}), bf16[4,128,768]{2,1,0:T(8,128)(2,1)S(1)}, u32[]{:S(2)}, u32[]{:S(2)}) async-start(bf16[4,128,768]{2,1,0:T(8,128)(2,1)} %broadcast_in_dim.193), calls=%async_computation.4 | async-start | bytes 1572864 | tf_op jit(solution)/shard_map/all_to_all | solution.py:620
  181.8 1.0 constant_dynamic-slice_fusion.3
  184.9 7.2 %all-to-all-done.4 = bf16[4,128,768]{2,1,0:T(8,128)(2,1)S(1)} async-done(((bf16[4,128,768]{2,1,0:T(8,128)(2,1)}), bf16[4,128,768]{2,1,0:T(8,128)(2,1)S(1)}, u32[]{:S(2)}, u32[]{:S(2)}) %all-to-all-start.4) | async-done | bytes 786464 | tf_op jit(solution)/shard_map/all_to_all | solution.py:620
  193.0 3.4 %prepare.1.packed = bf16[512,256]{1,0:T(8,128)(2,1)} custom-call(bf16[512,768]{1,0:T(8,128)(2,1)} %bitcast.69, bf16[256,768]{1,0:T(8,128)(2,1)} %pad.38.w_out, f32[512,256]{1,0:T(8,128)} %get-tuple-element.94.ctx, f32[2,768,1]{2,1,0:T(8,128)} %get-tuple-element.95.lse), custom_call_target="tpu_custom_call" | custom-call | flops 201326592 | bytes 1048576 | tf_op jit(solution)/shard_map/prepare/pallas_call | solution.py:401
  196.5 6.1 %weight_grads.1 = (f32[16,56,768]{2,1,0:T(8,128)}, bf16[16,56,768]{2,1,0:T(8,128)(2,1)}) custom-call(s32[1]{0:T(128)} %bitcast.core, bf16[512,768]{1,0:T(8,128)(2,1)} %get-tuple-element.83.h2, bf16[512,768]{1,0:T(8,128)(2,1)} %get-tuple-element.84.du, bf16[512,768]{1,0:T(8,128)(2,1)} %get-tuple-element.85.act, ...), custom_call_target="tpu_custom_call" | custom-call | flops 1207959552 | bytes 3538944 | tf_op jit(solution)/shard_map/weight_grads/pallas_call | solution.py:555
  202.6 3.3 %collective-permute-done = bf16[16,56,768]{2,1,0:T(8,128)(2,1)S(1)} collective-permute-done((bf16[16,56,768]{2,1,0:T(8,128)(2,1)}, bf16[16,56,768]{2,1,0:T(8,128)(2,1)S(1)}, u32[]{:S(2)}, u32[]{:S(2)}) %collective-permute-start) | collective-permute-done | bytes 1376288 | tf_op jit(solution)/shard_map/ppermute | solution.py:631
  206.0 3.2 add_convert_fusion
  209.1 21.3 %query_grad.1.d_query = bf16[512,256]{1,0:T(8,128)(2,1)} custom-call(s32[32]{0:T(128)} %select_reduce_fusion.slots, s32[2]{0:T(128)} %fusion.21.own, bf16[2,768,256]{2,1,0:T(8,128)(2,1)} %bitcast_select_fusion.2.q_heads, bf16[512,256]{1,0:T(8,128)(2,1)} %prepare.1.packed, bf16[8192,384]{1,0:T(8,128)(2,1)} %all-gather.8.cloned.1.call-done.kv), custom_call_target="tpu_custom_call" | custom-call | flops 19327352832 | bytes 6291456 | tf_op jit(solution)/shard_map/query_grad/pallas_call | solution.py:401
  230.4 1.7 all-gather.14.cloned.1.call-done.p_all
  232.1 8.9 %all-to-all-start.5 = ((bf16[16,56,768]{2,1,0:T(8,128)(2,1)}), bf16[16,56,768]{2,1,0:T(8,128)(2,1)S(1)}, u32[]{:S(2)}, u32[]{:S(2)}) async-start(bf16[16,56,768]{2,1,0:T(8,128)(2,1)} %add_convert_fusion), calls=%async_computation.5 | async-start | bytes 2752512 | tf_op jit(solution)/shard_map/all_to_all | solution.py:798
  241.0 16.6 %key_grad.1 = (bf16[512,256]{1,0:T(8,128)(2,1)}, bf16[512,192]{1,0:T(8,128)(2,1)}) custom-call(s32[32]{0:T(128)} %select_reduce_fusion.slots, s32[2]{0:T(128)} %fusion.21.own, bf16[2,768,256]{2,1,0:T(8,128)(2,1)} %get-tuple-element.98.k_heads, bf16[2,768,256]{2,1,0:T(8,128)(2,1)} %get-tuple-element.99.v_heads, ...), custom_call_target="tpu_custom_call" | custom-call | flops 25769803776 | bytes 6291456 | tf_op jit(solution)/shard_map/key_grad/pallas_call | solution.py:401
  257.6 2.5 all-to-all-done.5
  260.1 5.4 %finish.1 = (bf16[512,768]{1,0:T(8,128)(2,1)}, f32[16,32,640]{2,1,0:T(8,128)}, bf16[16,32,640]{2,1,0:T(8,128)(2,1)}) custom-call(s32[1]{0:T(128)} %bitcast.core, s32[1]{0:T(128)} %bitcast.1.me, bf16[512,256]{1,0:T(8,128)(2,1)} %query_grad.1.d_query, bf16[512,256]{1,0:T(8,128)(2,1)} %get-tuple-element.102.d_key, bf16[512,192]{1,0:T(8,128)(2,1)} %get-tuple-element.105.d_value, ...), custom_call_target="tpu_custom_call" | custom-call | flops 1006632960 | bytes 2949120 | tf_op jit(solution)/shard_map/finish/pallas_call | solution.py:401
  265.5 13.5 %collective-permute-start.1 = (bf16[16,32,640]{2,1,0:T(8,128)(2,1)}, bf16[16,32,640]{2,1,0:T(8,128)(2,1)S(1)}, u32[]{:S(2)}, u32[]{:S(2)}) collective-permute-start(bf16[16,32,640]{2,1,0:T(8,128)(2,1)} %get-tuple-element.111), channel_id=1, source_target_pairs={{0,4},{4,0},{1,5},{5,1},{2,6},{6,2},{3,7},{7,3},{8,12},{12,8},{9,1... | collective-permute-start | bytes 1966088 | tf_op jit(solution)/shard_map/ppermute | solution.py:631
  279.5 1.4 collective-permute-done.1
  280.9 2.3 add_convert_fusion.1
  283.2 1.2 pad_maximum_fusion
  284.4 1.0 dynamic-slice_bitcast_fusion.2
  286.0 2.0 collective-permute-start.3
  290.2 4.8 %all-to-all-start.6 = ((bf16[16,32,640]{2,1,0:T(8,128)(2,1)}), bf16[16,32,640]{2,1,0:T(8,128)(2,1)}, u32[]{:S(2)}, u32[]{:S(2)}) async-start(bf16[16,32,640]{2,1,0:T(8,128)(2,1)} %add_convert_fusion.1), calls=%async_computation.6 | async-start | bytes 1310720 | tf_op jit(solution)/shard_map/all_to_all | solution.py:807
  295.1 11.8 %collective-permute-done.2 = bf16[128,1536]{1,0:T(8,128)(2,1)} collective-permute-done((bf16[128,1536]{1,0:T(8,128)(2,1)}, bf16[128,1536]{1,0:T(8,128)(2,1)}, u32[]{:S(2)}, u32[]{:S(2)}) %collective-permute-start.2) | collective-permute-done | bytes 393248 | tf_op jit(solution)/shard_map/ppermute | solution.py:642
  307.5 1.4 fusion.1
  309.1 1.2 convert_reduce_fusion.4
  311.2 3.6 %all-to-all-start.7 = ((f32[4,6,1408]{2,1,0:T(8,128)}), f32[4,6,1408]{2,1,0:T(8,128)S(1)}, u32[]{:S(2)}, u32[]{:S(2)}) async-start(f32[4,6,1408]{2,1,0:T(8,128)} %concatenate.51), calls=%async_computation.7 | async-start | bytes 360448 | tf_op jit(solution)/shard_map/all_to_all | solution.py:826
  314.8 1.1 fusion.11
  315.9 5.2 %all-to-all-done.7 = f32[4,6,1408]{2,1,0:T(8,128)S(1)} async-done(((f32[4,6,1408]{2,1,0:T(8,128)}), f32[4,6,1408]{2,1,0:T(8,128)S(1)}, u32[]{:S(2)}, u32[]{:S(2)}) %all-to-all-start.7) | async-done | bytes 135200 | tf_op jit(solution)/shard_map/all_to_all | solution.py:826
  322.8 1.1 reshape.318
  (165 shorter events, 28.3 us)
Async XLA Ops:
  7.2 46.3 %all-gather.6.cloned.1.call-start = ((), (), s32[]{:S(2)}) async-start(), calls=%async_computation.8 | async-start | bytes 1966080 | tf_op jit(solution)/shard_map/all_gather | solution.py:706
  15.2 10.0 %all-to-all-start = ((bf16[4,6,640]{2,1,0:T(8,128)(2,1)}), bf16[4,6,640]{2,1,0:T(8,128)(2,1)S(1)}, u32[]{:S(2)}, u32[]{:S(2)}) async-start(bf16[4,6,640]{2,1,0:T(8,128)(2,1)} %copy.82), calls=%async_computation | async-start | bytes 81920 | tf_op jit(solution)/shard_map/all_to_all | solution.py:704
  19.6 78.0 %all-gather.8.cloned.1.call-start = ((), (), s32[]{:S(2)}) async-start(), calls=%async_computation.9 | async-start | bytes 6684672 | tf_op jit(solution)/shard_map/all_gather | solution.py:723
  53.5 4.0 %copy-start.13 = (s32[1,32]{1,0:T(1,128)S(1)}, s32[1,32]{1,0:T(1,128)}, u32[]{:S(2)}) copy-start(s32[1,32]{1,0:T(1,128)} %param.14) | copy-start | bytes 388
  53.5 8.9 %copy-start.10 = (bf16[1,6,3072]{2,1,0:T(8,128)(2,1)S(1)}, bf16[1,6,3072]{2,1,0:T(8,128)(2,1)}, u32[]{:S(2)}) copy-start(bf16[1,6,3072]{2,1,0:T(8,128)(2,1)} %param.21) | copy-start | bytes 110596
  57.3 5.7 %copy-start.12 = (bf16[1,6,768]{2,1,0:T(8,128)(2,1)S(1)}, bf16[1,6,768]{2,1,0:T(8,128)(2,1)}, u32[]{:S(2)}) copy-start(bf16[1,6,768]{2,1,0:T(8,128)(2,1)} %param.19) | copy-start | bytes 27652
  57.3 10.5 %copy-start.5 = (bf16[512,384]{1,0:T(8,128)(2,1)S(1)}, bf16[512,384]{1,0:T(8,128)(2,1)}, u32[]{:S(2)}) copy-start(bf16[512,384]{1,0:T(8,128)(2,1)} %get-tuple-element.71) | copy-start | bytes 1179652
  60.7 7.2 %copy-start.9 = (bf16[512,192]{1,0:T(8,128)(2,1)S(1)}, bf16[512,192]{1,0:T(8,128)(2,1)}, u32[]{:S(2)}) copy-start(bf16[512,192]{1,0:T(8,128)(2,1)} %get-tuple-element.70) | copy-start | bytes 589828
  63.7 9.1 %all-to-all-start.1 = ((bf16[4,6,1536]{2,1,0:T(8,128)(2,1)}), bf16[4,6,1536]{2,1,0:T(8,128)(2,1)S(1)}, u32[]{:S(2)}, u32[]{:S(2)}) async-start(bf16[4,6,1536]{2,1,0:T(8,128)(2,1)} %copy.85), calls=%async_computation.1 | async-start | bytes 196608 | tf_op jit(solution)/shard_map/all_to_all | solution.py:728
  67.1 79.6 %all-gather.10.cloned.1.call-start = ((), (), s32[]{:S(2)}) async-start(), calls=%async_computation.10 | async-start | bytes 3649536 | tf_op jit(solution)/shard_map/all_gather | solution.py:743
  70.3 2.6 copy-start.11
  97.7 94.4 %all-gather.12.cloned.1.call-start = ((), (), s32[]{:S(2)}) async-start(), calls=%async_computation.11 | async-start | bytes 4456448 | tf_op jit(solution)/shard_map/all_gather | solution.py:748
  157.2 5.2 %copy-start.1 = (bf16[4,192,512]{2,1,0:T(8,128)(2,1)S(1)}, bf16[4,192,512]{2,1,0:T(8,128)(2,1)}, u32[]{:S(2)}) copy-start(bf16[4,192,512]{2,1,0:T(8,128)(2,1)} %all_to_all.40) | copy-start | bytes 2359300
  157.2 5.5 %copy-start = (f32[128,768]{1,0:T(8,128)S(1)}, f32[128,768]{1,0:T(8,128)}, u32[]{:S(2)}) copy-start(f32[128,768]{1,0:T(8,128)} %get-tuple-element.86) | copy-start | bytes 1179652
  157.2 17.2 %all-to-all-start.3 = ((bf16[4,128,768]{2,1,0:T(8,128)(2,1)}), bf16[4,128,768]{2,1,0:T(8,128)(2,1)S(1)}, u32[]{:S(2)}, u32[]{:S(2)}) async-start(bf16[4,128,768]{2,1,0:T(8,128)(2,1)} %bitcast.78), calls=%async_computation.3 | async-start | bytes 1572864 | tf_op jit(solution)/shard_map/all_to_all | solution.py:626
  162.7 12.2 %copy-start.6 = (f32[128,768]{1,0:T(8,128)S(1)}, f32[128,768]{1,0:T(8,128)}, u32[]{:S(2)}) copy-start(f32[128,768]{1,0:T(8,128)} %param.25) | copy-start | bytes 1179652
  175.8 5.5 %copy-start.4 = (bf16[512,768]{1,0:T(8,128)(2,1)S(1)}, bf16[512,768]{1,0:T(8,128)(2,1)}, u32[]{:S(2)}) copy-start(bf16[512,768]{1,0:T(8,128)(2,1)} %get-tuple-element.84.du) | copy-start | bytes 2359300
  176.8 15.4 %all-to-all-start.4 = ((bf16[4,128,768]{2,1,0:T(8,128)(2,1)}), bf16[4,128,768]{2,1,0:T(8,128)(2,1)S(1)}, u32[]{:S(2)}, u32[]{:S(2)}) async-start(bf16[4,128,768]{2,1,0:T(8,128)(2,1)} %broadcast_in_dim.193), calls=%async_computation.4 | async-start | bytes 1572864 | tf_op jit(solution)/shard_map/all_to_all | solution.py:620
  180.3 51.8 %all-gather.14.cloned.1.call-start = ((), (), s32[]{:S(2)}) async-start(), calls=%async_computation.12 | async-start | bytes 4456448 | tf_op jit(solution)/shard_map/all_gather | solution.py:791
  192.1 0.9 copy-start.2
  202.6 3.3 %collective-permute-start = (bf16[16,56,768]{2,1,0:T(8,128)(2,1)}, bf16[16,56,768]{2,1,0:T(8,128)(2,1)S(1)}, u32[]{:S(2)}, u32[]{:S(2)}) collective-permute-start(bf16[16,56,768]{2,1,0:T(8,128)(2,1)} %get-tuple-element.92), channel_id=1, source_target_pairs={{0,4},{4,0},{1,5},{5,1},{2,6},{6,2},{3,7},{7,3},{8,12},{12,8},{9,1... | collective-permute-start | bytes 4128776 | tf_op jit(solution)/shard_map/ppermute | solution.py:631
  232.1 28.0 %all-to-all-start.5 = ((bf16[16,56,768]{2,1,0:T(8,128)(2,1)}), bf16[16,56,768]{2,1,0:T(8,128)(2,1)S(1)}, u32[]{:S(2)}, u32[]{:S(2)}) async-start(bf16[16,56,768]{2,1,0:T(8,128)(2,1)} %add_convert_fusion), calls=%async_computation.5 | async-start | bytes 2752512 | tf_op jit(solution)/shard_map/all_to_all | solution.py:798
  260.1 18.9 %copy-start.3 = (bf16[128,768]{1,0:T(8,128)(2,1)S(1)}, bf16[128,768]{1,0:T(8,128)(2,1)}, u32[]{:S(2)}) copy-start(bf16[128,768]{1,0:T(8,128)(2,1)} %param.13) | copy-start | bytes 589828
  265.5 15.4 %collective-permute-start.1 = (bf16[16,32,640]{2,1,0:T(8,128)(2,1)}, bf16[16,32,640]{2,1,0:T(8,128)(2,1)S(1)}, u32[]{:S(2)}, u32[]{:S(2)}) collective-permute-start(bf16[16,32,640]{2,1,0:T(8,128)(2,1)} %get-tuple-element.111), channel_id=1, source_target_pairs={{0,4},{4,0},{1,5},{5,1},{2,6},{6,2},{3,7},{7,3},{8,12},{12,8},{9,1... | collective-permute-start | bytes 1966088 | tf_op jit(solution)/shard_map/ppermute | solution.py:631
  279.4 3.7 %copy-start.8 = (bf16[512,768]{1,0:T(8,128)(2,1)S(1)}, bf16[512,768]{1,0:T(8,128)(2,1)}, u32[]{:S(2)}) copy-start(bf16[512,768]{1,0:T(8,128)(2,1)} %get-tuple-element.112) | copy-start | bytes 2359300
  285.5 21.3 %collective-permute-start.2 = (bf16[128,1536]{1,0:T(8,128)(2,1)}, bf16[128,1536]{1,0:T(8,128)(2,1)}, u32[]{:S(2)}, u32[]{:S(2)}) collective-permute-start(bf16[128,1536]{1,0:T(8,128)(2,1)} %get-tuple-element.180), channel_id=1, source_target_pairs={{0,1},{1,2},{2,3},{3,0},{4,5},{5,6},{6,7},{7,4},{8,9},{9,10},{10,1... | collective-permute-start | bytes 1179656 | tf_op jit(solution)/shard_map/ppermute | solution.py:642
  286.0 20.8 %collective-permute-start.3 = (bf16[128,1536]{1,0:T(8,128)(2,1)}, bf16[128,1536]{1,0:T(8,128)(2,1)}, u32[]{:S(2)}, u32[]{:S(2)}) collective-permute-start(bf16[128,1536]{1,0:T(8,128)(2,1)} %get-tuple-element.182), channel_id=1, source_target_pairs={{0,2},{1,3},{2,0},{3,1},{4,6},{5,7},{6,4},{7,5},{8,10},{9,11},{10,... | collective-permute-start | bytes 1179656 | tf_op jit(solution)/shard_map/ppermute | solution.py:642
  288.1 19.4 %collective-permute-start.4 = (bf16[128,1536]{1,0:T(8,128)(2,1)}, bf16[128,1536]{1,0:T(8,128)(2,1)}, u32[]{:S(2)}, u32[]{:S(2)}) collective-permute-start(bf16[128,1536]{1,0:T(8,128)(2,1)} %get-tuple-element.181), channel_id=1, source_target_pairs={{0,3},{1,0},{2,1},{3,2},{4,7},{5,4},{6,5},{7,6},{8,11},{9,8},{10,9... | collective-permute-start | bytes 1179656 | tf_op jit(solution)/shard_map/ppermute | solution.py:642
  290.2 18.9 %all-to-all-start.6 = ((bf16[16,32,640]{2,1,0:T(8,128)(2,1)}), bf16[16,32,640]{2,1,0:T(8,128)(2,1)}, u32[]{:S(2)}, u32[]{:S(2)}) async-start(bf16[16,32,640]{2,1,0:T(8,128)(2,1)} %add_convert_fusion.1), calls=%async_computation.6 | async-start | bytes 1310720 | tf_op jit(solution)/shard_map/all_to_all | solution.py:807
  308.9 5.9 %copy-start.7 = (f32[128,768]{1,0:T(8,128)S(1)}, f32[128,768]{1,0:T(8,128)}, u32[]{:S(2)}) copy-start(f32[128,768]{1,0:T(8,128)} %get-tuple-element.177) | copy-start | bytes 1179652
  311.2 9.8 %all-to-all-start.7 = ((f32[4,6,1408]{2,1,0:T(8,128)}), f32[4,6,1408]{2,1,0:T(8,128)S(1)}, u32[]{:S(2)}, u32[]{:S(2)}) async-start(f32[4,6,1408]{2,1,0:T(8,128)} %concatenate.51), calls=%async_computation.7 | async-start | bytes 360448 | tf_op jit(solution)/shard_map/all_to_all | solution.py:826
Sparse Core Ops, SparseCore 0:
  14.7 28.8 all-gather.5
  57.5 40.1 all-gather.7
  100.6 45.9 all-gather.9
  148.2 37.3 all-gather.11
  196.6 35.4 all-gather.13
